TPU v7x, 32 devices: a whole 2x2x4 slice. The times are simulated.
32 devices in a mesh: ctx: 16 (over z, x, core), tp: 2 (over y).
Axes of the slice: x: 2, y: 2, z: 4, core: 2. Of those that a mesh axis runs over, the one named last changes fastest.
Arguments:
- tokens: bfloat16 [1920, 8192], P('tp', 'ctx'), may hold values from -6 to 6
- norm_gain: float32 [1920], replicated, may hold values from 0.1 to 1.9
- w_in: bfloat16 [3, 1920, 1920], P(None, 'tp'), may hold values from -0.125 to 0.125
- w_short: float32 [3, 3, 1920], P(None, None, 'tp'), may hold values from -3 to 3
- decay_rate: float32 [16, 1920], P(None, 'tp'), as said below
- residue: float32 [16, 1920], P(None, 'tp'), may hold values from -1.5 to 1.5
- skip_gain: float32 [1920], P('tp'), may hold values from -3 to 3
- w_out: bfloat16 [1920, 1920], P('tp'), may hold values from -0.125 to 0.125
Outputs:
- mixed: bfloat16 [1920, 8192], P('tp', 'ctx')
Inputs may be any that keep to these rules, and one draw needn't show every extreme that they name: `decay_rate`: every rate lies between 0.2 / 8192 and 1 / 30.
All inputs are finite; a program needn't handle non-finite values.
Results may differ from a plain program's by a relative error of at most 0.0077.
Values may be sent and summed in bfloat16 or wider, within the bound.
No kernel may reach another device: no remote copies, remote signals or barrier semaphores. Data moves between devices by JAX's collectives and lax.ppermute only.
A program may use at most 256 MiB of HBM per device.

v0:
```python
import functools

import jax
import jax.numpy as jnp
from jax import lax
from jax.experimental import pallas as pl
from jax.experimental.pallas import tpu as pltpu
from jax.sharding import PartitionSpec as P


F32 = jnp.float32
BF16 = jnp.bfloat16
ROWS = 8
LANES = 128
BLOCK = 256
CHUNKS = 4
SPAN = 16
VMEM_LIMIT = 10 * 2**20
CONTRACT_LAST = (((1,), (1,)), ((), ()))
CONTRACT_FIRST = (((0,), (0,)), ((), ()))


def lane_groups(low, width):
    return [(start, min(LANES, low + width - start)) for start in range(low, low + width, LANES)]


def rows_as(row, width):
    return jnp.broadcast_to(row, (ROWS, width))


def tree_sum(terms):
    while len(terms) > 1:
        terms = [sum(terms[k + 1 : k + 2], terms[k]) for k in range(0, len(terms), 2)]
    return terms[0]


def token_picker(first_row, rows, tokens):
    length = tokens // ROWS
    row = lax.broadcasted_iota(jnp.int32, (rows, tokens), 0)
    column = lax.broadcasted_iota(jnp.int32, (rows, tokens), 1)
    wanted = lax.rem(row, ROWS) * length + lax.div(row, ROWS) + first_row // ROWS
    return jnp.where(column == wanted, 1.0, 0.0).astype(BF16)


def turned(pick, tokens):
    return lax.dot_general(pick, tokens, CONTRACT_LAST, preferred_element_type=F32).astype(BF16)


def first_rows(halo, tokens_ref, out_ref, edge_ref):
    tokens = tokens_ref.shape[1]
    out_ref[...] = turned(token_picker(-halo, out_ref.shape[0], tokens), tokens_ref[...])
    row = lax.broadcasted_iota(jnp.int32, (halo, tokens), 0)
    column = lax.broadcasted_iota(jnp.int32, (halo, tokens), 1)
    wanted = jnp.where(lax.rem(row, ROWS) == 0, tokens - halo // ROWS + lax.div(row, ROWS), -1)
    edge_ref[...] = turned(jnp.where(column == wanted, 1.0, 0.0).astype(BF16), tokens_ref[...])


def next_rows(row, tokens_ref, *chunk_refs):
    tokens = tokens_ref.shape[1]
    for ref in chunk_refs:
        ref[...] = turned(token_picker(row, ref.shape[0], tokens), tokens_ref[...])
        row += ref.shape[0]


def join_edge(edge_ref, chunk_ref, out_ref):
    halo = edge_ref.shape[0]
    out_ref[:halo, :] = edge_ref[...]
    out_ref[halo:, :] = chunk_ref[...]


def load_weights(places, w_hbm, out_ref, w_ref, sem):
    copies = [
        pltpu.make_async_copy(w_hbm.at[place], w_ref.at[place], sem.at[k])
        for k, place in enumerate(places)
    ]
    for copy in copies:
        copy.start()
    for (s, part), copy in zip(places, copies):
        copy.wait()
        out_ref[s, :, part] = w_ref[s, part, :].T


def short_conv(p_ref, short_ref, s, part, rows, taps):
    width = part.stop - part.start
    total = None
    for offset in range(taps):
        start = ROWS * (taps - 1 - offset)
        term = short_ref[offset, s : s + 1, part] * p_ref[start : start + rows, :width]
        total = term if total is None else total + term
    return total


def project(normed, w_ref, s, part):
    product = jnp.dot(normed, w_ref[s, :, part], preferred_element_type=F32)
    return product.astype(BF16).astype(F32)


def signal_stage(pieces, chunks, first, last, row, taps, *refs):
    refs = list(refs)
    me_ref = refs.pop(0)
    token_refs = [[refs.pop(0) for _ in range(pieces)] for _ in range(chunks)]
    if not first:
        _, _, _, states_in, tail_in = [refs.pop(0) for _ in range(5)]
    gain_ref, w_ref, short_ref, rate_ref = refs[:4]
    normed_ref, signal_ref, marks_ref, states_ref, tail_ref = refs[4:9]
    total_ref = refs[9] if last else None
    x_ref, p_ref = refs[-2:]
    halo = ROWS * (taps - 1)
    modes, channels = rate_ref.shape
    read, share = x_ref.shape[0], token_refs[0][0].shape[1]
    rows = read - halo if first else read
    length = signal_ref.shape[0] // ROWS
    me = me_ref[0]

    values = []
    for s in range(pieces):
        value = [refs_of[s][...].astype(F32) for refs_of in token_refs]
        if first:
            front, edge = value[0][:halo], value[-1][:halo]
            value = [front + edge, value[0][halo:], *value[1:-1], value[-1][halo:]]
        values.append(jnp.concatenate(value, axis=0) if len(value) > 1 else value[0])
    for rank in range(pieces):
        chosen = values[0]
        for s in range(1, pieces):
            chosen = jnp.where(me == (rank - s) % pieces, values[s], chosen)
        x_ref[:, rank * share : (rank + 1) * share] = chosen
    features = x_ref[...]
    mean = jnp.mean(features * features, axis=1, keepdims=True)
    normed = (features * lax.rsqrt(mean + 1e-06) * gain_ref[...]).astype(BF16)
    begin = 0 if first else halo + row
    normed_ref[begin : begin + read, :] = normed

    for low in range(0, channels, BLOCK):
        width = min(BLOCK, channels - low)
        part = slice(low, low + width)
        for s in (1, 2):
            if not first:
                p_ref[:halo, :width] = tail_in[s - 1, :, part]
            p_ref[halo + rows - read :, :width] = project(
                normed_ref[begin : begin + read, :], w_ref, s, part
            )
            tail_ref[s - 1, :, part] = p_ref[rows:, :width]
            short = short_conv(p_ref, short_ref, s, part, rows, taps)
            if s == 1:
                signal_ref[row : row + rows, part] = short
            else:
                signal_ref[row : row + rows, part] = signal_ref[row : row + rows, part] * short
        for start, size in lane_groups(low, width):
            lanes = slice(start, start + size)
            rate = [rows_as(rate_ref[n : n + 1, lanes], size) for n in range(modes)]
            decay = [jnp.exp(-r) for r in rate]

            if first:
                states = (jnp.zeros((ROWS, size), F32),) * modes
            else:
                states = tuple(states_in[n, :, lanes] for n in range(modes))
            for at in range(row, row + rows, SPAN * ROWS):
                mark = at // (SPAN * ROWS)
                for n in range(modes):
                    marks_ref[mark, n, :, lanes] = states[n]

                def step(i, states):
                    here = pl.ds(pl.multiple_of(at + i * ROWS, ROWS), ROWS)
                    now = signal_ref[here, lanes]
                    return tuple(states[n] * decay[n] + now for n in range(modes))

                states = lax.fori_loop(0, SPAN, step, states, unroll=8)
            for n in range(modes):
                states_ref[n, :, lanes] = states[n]
            if last:
                left = lax.broadcasted_iota(jnp.int32, (ROWS, size), 0)
                left = ((ROWS - 1 - left) * length).astype(F32)
                for n in range(modes):
                    total_ref[n : n + 1, lanes] = jnp.sum(
                        states[n] * jnp.exp(-rate[n] * left), axis=0, keepdims=True
                    )


def local_stage(row, rows, taps, *refs):
    normed_ref, signal_ref, states_ref, w_ref, short_ref, rate_ref, mode_ref, skip_ref = refs[:8]
    q_ref, local_ref = refs[8:10]
    begin_ref = refs[10] if row == 0 else None
    p_ref = refs[-1]
    modes, channels = rate_ref.shape
    length = signal_ref.shape[0] // ROWS
    for low in range(0, channels, BLOCK):
        width = min(BLOCK, channels - low)
        part = slice(low, low + width)
        normed = normed_ref[row : row + p_ref.shape[0], :]
        p_ref[:, :width] = project(normed, w_ref, 0, part)
        q_ref[:, part] = short_conv(p_ref, short_ref, 0, part, rows, taps)
        for start, size in lane_groups(low, width):
            lanes = slice(start, start + size)
            rate = [rows_as(rate_ref[n : n + 1, lanes], size) for n in range(modes)]
            segment = lax.broadcasted_iota(jnp.int32, (ROWS, size), 0)
            if row == 0:
                for n in range(modes):
                    run = states_ref[n, :, lanes]
                    for hop in (1, 2, 4):
                        weight = jnp.where(segment >= hop, jnp.exp(-rate[n] * (hop * length)), 0.0)
                        run = run + weight * pltpu.roll(run, hop, 0)
                    begin_ref[n, :, lanes] = jnp.where(segment >= 1, pltpu.roll(run, 1, 0), 0.0)
            lag = segment.astype(F32)
            filters = []
            for first_lag in range(0, SPAN, ROWS):
                values = tree_sum(
                    [
                        rows_as(mode_ref[n : n + 1, lanes], size)
                        * jnp.exp(-rate[n] * (lag + first_lag))
                        for n in range(modes)
                    ]
                )
                filters += [rows_as(values[j : j + 1, :], size) for j in range(ROWS)]
            filters[0] = filters[0] + skip_ref[:, lanes]

            def span(i, carry):
                base = i * (SPAN * ROWS)
                now = [
                    signal_ref[pl.ds(pl.multiple_of(row + base + k * ROWS, ROWS), ROWS), lanes]
                    for k in range(SPAN)
                ]
                for k in range(SPAN):
                    local_ref[pl.ds(pl.multiple_of(base + k * ROWS, ROWS), ROWS), lanes] = tree_sum(
                        [filters[j] * now[k - j] for j in range(k + 1)]
                    )
                return carry

            lax.fori_loop(0, rows // (SPAN * ROWS), span, 0)


def second_stage(pieces, row, rows, length, *refs):
    me_ref, q_ref, local_ref, begin_ref, marks_ref, carry_ref, rate_ref, mode_ref, w_ref = refs[:9]
    send_ref, own_ref, gated_ref = refs[9:]
    modes, channels = rate_ref.shape
    for start, size in lane_groups(0, channels):
        lanes = slice(start, start + size)
        rate = [rows_as(rate_ref[n : n + 1, lanes], size) for n in range(modes)]
        decay = [jnp.exp(-r) for r in rate]
        segment = lax.broadcasted_iota(jnp.int32, (ROWS, size), 0)
        past = (segment * length).astype(F32)
        for at in range(row, row + rows, SPAN * ROWS):
            mark = at // (SPAN * ROWS)
            states = []
            for n in range(modes):
                state = begin_ref[n, :, lanes] + jnp.exp(-rate[n] * past) * carry_ref[
                    n : n + 1, lanes
                ]
                if mark > 0:
                    state = marks_ref[mark, n, :, lanes] + state * jnp.exp(-rate[n] * (SPAN * mark))
                states.append(mode_ref[n : n + 1, lanes] * state)

            def step(i, states):
                here = pl.ds(pl.multiple_of(at - row + i * ROWS, ROWS), ROWS)
                states = tuple(states[n] * decay[n] for n in range(modes))
                gated_ref[here, lanes] = q_ref[here, lanes] * tree_sum(
                    [local_ref[here, lanes]] + list(states)
                )
                return states

            lax.fori_loop(0, SPAN, step, tuple(states), unroll=4)
    product = jnp.dot(gated_ref[...].astype(BF16), w_ref[...], preferred_element_type=F32)
    share = own_ref.shape[1]
    me = me_ref[0]
    columns = [product[:, rank * share : (rank + 1) * share] for rank in range(pieces)]
    for s in range(pieces):
        chosen = columns[0]
        for rank in range(1, pieces):
            chosen = jnp.where(me == (rank - s) % pieces, columns[rank], chosen)
        if s == 0:
            own_ref[...] = chosen
        else:
            send_ref[(s - 1) * rows : s * rows, :] = chosen.astype(BF16)


def last_stage(pieces, sizes, row, more, *refs):
    chunks = len(sizes)
    own_refs, came_refs = refs[:chunks], refs[chunks : chunks * pieces]
    done_ref = refs[chunks * pieces] if more else None
    out_ref, mixed_ref = refs[-2:]
    at = 0
    for j, size in enumerate(sizes):
        total = own_refs[j][...]
        for s in range(pieces - 1):
            total = total + came_refs[j * (pieces - 1) + s][...].astype(F32)
        mixed_ref[at : at + size, :] = total.astype(BF16)
        at += size
    pick = token_picker(row, at, out_ref.shape[1])
    out = lax.dot_general(mixed_ref[...], pick, CONTRACT_FIRST, preferred_element_type=F32)
    if more:
        out = out + done_ref[...]
    out_ref[...] = out.astype(out_ref.dtype)


def call(kernel, name, scalars, operands, outs, scratch, aliases={}):
    vmem = pl.BlockSpec(memory_space=pltpu.VMEM)
    smem = pl.BlockSpec(memory_space=pltpu.SMEM)
    return pl.pallas_call(
        kernel,
        out_shape=outs,
        in_specs=[smem] * len(scalars) + [vmem] * len(operands),
        out_specs=[vmem] * len(outs),
        scratch_shapes=scratch,
        input_output_aliases=aliases,
        compiler_params=pltpu.CompilerParams(vmem_limit_bytes=VMEM_LIMIT),
        cost_estimate=pl.CostEstimate(flops=1, bytes_accessed=1, transcendentals=0),
        name=name,
    )(*scalars, *operands)


def in_vmem(w):
    streams, channels, features = w.shape
    block = min(BLOCK, channels)
    places = [
        (s, slice(low, min(low + block, channels)))
        for s in (1, 2, 0)
        for low in range(0, channels, block)
    ]
    return pl.pallas_call(
        functools.partial(load_weights, places),
        out_shape=pltpu.VMEM((streams, features, channels), w.dtype),
        in_specs=[pl.BlockSpec(memory_space=pl.ANY)],
        out_specs=pl.BlockSpec(memory_space=pltpu.VMEM),
        scratch_shapes=[
            pltpu.VMEM(w.shape, w.dtype),
            pltpu.SemaphoreType.DMA((len(places),)),
        ],
        compiler_params=pltpu.CompilerParams(vmem_limit_bytes=46 * 2**20),
        cost_estimate=pl.CostEstimate(flops=1, bytes_accessed=1, transcendentals=0),
        name="load_weights",
    )(w)


def run_signal(pieces, row, count, first, last, taps, place, tokens, before, gain, w_in, w_short, rate):
    streams, features, channels = w_in.shape
    modes = rate.shape[0]
    halo = ROWS * (taps - 1)
    read = sum(chunk[0].shape[0] for chunk in tokens) - (halo if first else 0)
    rows = read - halo if first else read
    outs = [
        jax.ShapeDtypeStruct((halo + count, features), BF16),
        jax.ShapeDtypeStruct((count, channels), F32),
        jax.ShapeDtypeStruct((count // (SPAN * ROWS), modes, ROWS, channels), F32),
        jax.ShapeDtypeStruct((modes, ROWS, channels), F32),
        jax.ShapeDtypeStruct((streams - 1, halo, channels), F32),
    ]
    if last:
        outs.append(jax.ShapeDtypeStruct((modes, channels), F32))
    inputs = 1 + len(tokens) * pieces
    return call(
        functools.partial(signal_stage, pieces, len(tokens), first, last, row, taps),
        "signal_stage",
        [place],
        [part for chunk in tokens for part in chunk] + list(before) + [gain, w_in, w_short, rate],
        outs,
        [
            pltpu.VMEM((read, features), F32),
            pltpu.VMEM((halo + rows, min(BLOCK, channels)), F32),
        ],
        aliases={} if first else {inputs + k: k for k in range(3)},
    )


def run_local(row, rows, taps, normed, signal, states, w_in, w_short, rate, mode, skip):
    channels = signal.shape[1]
    out = jax.ShapeDtypeStruct((rows, channels), F32)
    begin = jax.ShapeDtypeStruct(states.shape, F32)
    return call(
        functools.partial(local_stage, row, rows, taps),
        "local_stage",
        [],
        [normed, signal, states, w_in, w_short, rate, mode, skip],
        [out, out] + ([begin] if row == 0 else []),
        [pltpu.VMEM((rows + ROWS * (taps - 1), min(BLOCK, channels)), F32)],
    )


def run_second(pieces, row, rows, count, place, q, local, begin, marks, carry, rate, mode, w):
    channels, features = w.shape
    share = features // pieces
    return call(
        functools.partial(second_stage, pieces, row, rows, count // ROWS),
        "second_stage",
        [place],
        [q, local, begin, marks, carry, rate, mode, w],
        [
            jax.ShapeDtypeStruct((max(1, pieces - 1) * rows, share), BF16),
            jax.ShapeDtypeStruct((rows, share), F32),
        ],
        [pltpu.VMEM((rows, channels), F32)],
    )


def run_last(pieces, sizes, row, own, came, done, count):
    share = own[0].shape[1]
    rows = sum(sizes)
    (out,) = call(
        functools.partial(last_stage, pieces, sizes, row, bool(done)),
        "last_stage",
        [],
        [*own, *came, *done],
        [jax.ShapeDtypeStruct((share, count), BF16 if row + rows == count else F32)],
        [pltpu.VMEM((rows, share), BF16)],
    )
    return out


def rotate(value, axis, steps):
    count = lax.axis_size(axis)
    return lax.ppermute(value, axis, [((i + steps) % count, i) for i in range(count)])


def combine_states(span, stride, radix, count, *refs):
    place_ref, rate_ref, total_ref = refs[:3]
    others = refs[3 : 2 + radix]
    refs = refs[2 + radix :]
    carry_in = refs[0] if stride > 1 else None
    carry_ref = refs[1] if stride > 1 else refs[0]
    position = place_ref[1]
    digit = lax.rem(lax.div(position, stride), radix)
    inner = lax.rem(position, stride)
    unit = span * stride
    rate = rate_ref[...]
    before = jnp.zeros(rate.shape, F32)
    for shift in range(1, radix):
        reached = jnp.where(digit >= shift, 1.0, 0.0)
        before = before + jnp.exp(-rate * (unit * (shift - 1))) * (others[shift - 1][...] * reached)
    if stride > 1:
        carry_ref[...] = carry_in[...] + jnp.exp(-rate * (span * inner).astype(F32)) * before
    else:
        carry_ref[...] = before
    if stride * radix < count:
        new = jnp.exp(-rate * (unit * (radix - 1 - digit)).astype(F32)) * total_ref[...]
        for shift in range(1, radix):
            at = lax.rem(digit - shift + radix, radix)
            weight = jnp.exp(-rate * (unit * (radix - 1 - at)).astype(F32))
            new = new + weight * others[shift - 1][...]
        refs[-1][...] = new


def carried_in(state, rate, span, axis, place, between):
    count = lax.axis_size(axis)
    total, stride, carry = state, 1, []
    while stride < count:
        radix = 4 if count % (stride * 4) == 0 else 2
        assert count % (stride * radix) == 0
        group = stride * radix
        others = []
        for shift in range(1, radix):
            pairs = []
            for i in range(count):
                digit = (i // stride) % radix
                pairs.append((i + ((digit - shift) % radix - digit) * stride, i))
            others.append(lax.ppermute(total, axis, pairs))
        others = between(others)
        shape = jax.ShapeDtypeStruct(state.shape, F32)
        carry = call(
            functools.partial(combine_states, span, stride, radix, count),
            "combine_states",
            [place],
            [rate, total, *others, *carry],
            [shape] * (2 if group < count else 1),
            [],
        )
        if group < count:
            *carry, total = carry
        stride = group
    return carry[0]


def body(tokens, norm_gain, w_in, w_short, decay_rate, residue, skip_gain, w_out):
    pieces, count = lax.axis_size("tp"), lax.axis_size("ctx")
    share, rows = tokens.shape
    channels = w_in.shape[1]
    taps = w_short.shape[0]
    halo = ROWS * (taps - 1)
    sizes = [rows // CHUNKS] * CHUNKS
    bf16_rows = lambda size: jax.ShapeDtypeStruct((size, share), BF16)

    place = jnp.stack([lax.axis_index("tp"), lax.axis_index("ctx")]).astype(jnp.int32)
    tokens, place = lax.optimization_barrier((tokens, place))
    x0, edge = call(
        functools.partial(first_rows, halo), "first_rows", [], [tokens],
        [bf16_rows(halo + sizes[0]), bf16_rows(halo)], [],
    )
    edge = lax.ppermute(edge, "ctx", [(i, i + 1) for i in range(lax.axis_size("ctx") - 1)])
    x1, *others = call(
        functools.partial(next_rows, sizes[0]), "next_rows", [], [tokens],
        [bf16_rows(size) for size in sizes[1:]], [],
    )
    (x1,) = call(join_edge, "join_edge", [], [edge, x1], [bf16_rows(halo + sizes[1])], [])
    x1, others = lax.optimization_barrier((x1, others))
    x = [x0, x1, *others]
    residue, norm_gain, skip_gain, *_ = lax.optimization_barrier((residue, norm_gain, skip_gain, *x))
    mode = residue * jnp.sqrt(-jnp.expm1(-2.0 * decay_rate))
    gain = norm_gain[None, :]
    skip = skip_gain[None, :]
    parts = [[part] + [rotate(part, "tp", s) for s in range(1, pieces)] for part in x]
    w_in, mode, gain, skip, *_ = lax.optimization_barrier((w_in, mode, gain, skip, *x))
    w_in = pltpu.with_memory_space_constraint(in_vmem(w_in), pltpu.VMEM)

    before, row = [], 0
    for group in [[0, 1]] + [[j] for j in range(2, CHUNKS)]:
        results = run_signal(
            pieces, row, rows, group[0] == 0, group[-1] == CHUNKS - 1, taps, place,
            [parts[j] for j in group], before, gain, w_in, w_short, decay_rate,
        )
        before = results[:5]
        row += sum(sizes[j] for j in group)
    normed, signal, marks, states, _ = before
    state, normed, signal, states = lax.optimization_barrier((results[5], normed, signal, states))
    out_sizes = [rows // 4, rows // 2, rows // 4]
    out_rows = [0, rows // 4, 3 * rows // 4]
    small = [w_in, w_short, decay_rate, mode, skip]
    done = []

    def local_part():
        k = len(done)
        done.append(run_local(out_rows[k], out_sizes[k], taps, normed, signal, states, *small))

    def between(others):
        if len(done) < 2:
            local_part()
            others, done[-1] = lax.optimization_barrier((others, done[-1]))
        return others

    carry = carried_in(state, decay_rate, rows, "ctx", place, between)
    while len(done) < 2:
        local_part()
    begin = done[0][2]
    own, came = [], []
    for j in range(len(out_sizes)):
        if j == 2:
            normed, signal, came[: pieces - 1] = lax.optimization_barrier(
                (normed, signal, came[: pieces - 1])
            )
            local_part()
        send, kept = run_second(
            pieces, out_rows[j], out_sizes[j], rows, place, *done[j][:2], begin, marks, carry,
            decay_rate, mode, w_out,
        )
        own.append(kept)
        for s in range(1, pieces):
            came.append(rotate(send[(s - 1) * out_sizes[j] : s * out_sizes[j]], "tp", -s))
    early = out_rows[-1]
    cut = (len(out_sizes) - 1) * (pieces - 1)
    done = run_last(pieces, out_sizes[:-1], 0, own[:-1], came[:cut], [], rows)
    return run_last(pieces, out_sizes[-1:], early, own[-1:], came[cut:], [done], rows)


def solution(mesh):
    placed = (
        P("tp", "ctx"),
        P(),
        P(None, "tp", None),
        P(None, None, "tp"),
        P(None, "tp"),
        P(None, "tp"),
        P("tp"),
        P("tp", None),
    )
    return jax.shard_map(
        body, mesh=mesh, in_specs=placed, out_specs=P("tp", "ctx"), check_vma=False
    )
```

profile of v0, /device:TPU:0, one launch (start us, length us, event | category | flops | bytes accessed | tf_op | source)
XLA Modules:
  0.0 81.6 jit_solution(5561089737062996578)
XLA Ops:
  0.0 0.1 pad_add_fusion.refs_0_
  0.1 1.2 %copy-done.2 = bf16[960,512]{1,0:T(8,128)(2,1)S(1)} copy-done((bf16[960,512]{1,0:T(8,128)(2,1)S(1)}, bf16[960,512]{1,0:T(8,128)(2,1)}, u32[]{:S(2)}) %copy-start.2) | copy-done | bytes 983064
  1.3 0.7 first_rows.1
  1.9 2.4 %collective-permute-start = (bf16[16,960]{1,0:T(8,128)(2,1)S(1)}, bf16[16,960]{1,0:T(8,128)(2,1)S(1)}, u32[]{:S(2)}, u32[]{:S(2)}) collective-permute-start(bf16[16,960]{1,0:T(8,128)(2,1)S(1)} %get-tuple-element.72), channel_id=1, source_target_pairs={{0,2},{2,4},{4,6},{6,8},{8,10},{10,12},{12,14},{14,16},{16,18},{18... | collective-permute-start | bytes 92168 | tf_op jit(solution)/shard_map/ppermute | solution.py:485
  4.3 2.4 %collective-permute-start.3 = (bf16[144,960]{1,0:T(8,128)(2,1)S(1)}, bf16[144,960]{1,0:T(8,128)(2,1)S(1)}, u32[]{:S(2)}, u32[]{:S(2)}) collective-permute-start(bf16[144,960]{1,0:T(8,128)(2,1)S(1)} %get-tuple-element.78.refs_1_), channel_id=1, source_target_pairs={{1,0},{0,1},{3,2},{2,3},{5,4},{4,5},{7,6},{6,7},{9,8},{8,9},{11,10... | collective-permute-start | bytes 829448 | tf_op jit(solution)/shard_map/ppermute | solution.py:409
  6.7 1.0 %next_rows.1 = (bf16[128,960]{1,0:T(8,128)(2,1)S(1)}, bf16[128,960]{1,0:T(8,128)(2,1)S(1)}, bf16[128,960]{1,0:T(8,128)(2,1)S(1)}) custom-call(bf16[960,512]{1,0:T(8,128)(2,1)S(1)} %copy-done.2), custom_call_target="tpu_custom_call" | custom-call | flops 1 | bytes 1 | tf_op jit(solution)/shard_map/next_rows/pallas_call | solution.py:297
  7.8 0.0 collective-permute-done.edge_ref
  7.8 0.1 collective-permute-start.4
  7.9 2.0 %collective-permute-start.2 = (bf16[128,960]{1,0:T(8,128)(2,1)S(1)}, bf16[128,960]{1,0:T(8,128)(2,1)S(1)}, u32[]{:S(2)}, u32[]{:S(2)}) collective-permute-start(bf16[128,960]{1,0:T(8,128)(2,1)S(1)} %get-tuple-element.77.refs_1_), channel_id=1, source_target_pairs={{1,0},{0,1},{3,2},{2,3},{5,4},{4,5},{7,6},{6,7},{9,8},{8,9},{11,10... | collective-permute-start | bytes 737288 | tf_op jit(solution)/shard_map/ppermute | solution.py:409
  9.9 0.1 collective-permute-start.1
  10.0 0.0 copy-done.6
  10.1 0.0 copy-start.3
  10.1 5.3 %load_weights.1.refs_6_.refs_9_.refs_3_ = bf16[3,1920,960]{2,1,0:T(8,128)(2,1)S(1)} custom-call(bf16[3,960,1920]{2,1,0:T(8,128)(2,1)} %w_hbm), custom_call_target="tpu_custom_call" | custom-call | flops 1 | bytes 1 | tf_op jit(solution)/shard_map/load_weights/pallas_call | solution.py:318
  15.4 0.0 collective-permute-done.3.refs_2_
  15.4 4.3 %collective-permute-done.4.refs_4_ = bf16[144,960]{1,0:T(8,128)(2,1)S(1)} collective-permute-done((bf16[144,960]{1,0:T(8,128)(2,1)S(1)}, bf16[144,960]{1,0:T(8,128)(2,1)S(1)}, u32[]{:S(2)}, u32[]{:S(2)}) %collective-permute-start.4) | collective-permute-done | bytes 276512 | tf_op jit(solution)/shard_map/ppermute | solution.py:409
  19.7 5.9 %signal_stage.3 = (bf16[528,1920]{1,0:T(8,128)(2,1)S(1)}, f32[512,960]{1,0:T(8,128)S(1)}, f32[4,16,8,960]{3,2,1,0:T(8,128)S(1)}, f32[16,8,960]{2,1,0:T(8,128)S(1)}, f32[2,16,960]{2,1,0:T(8,128)S(1)}) custom-call(s32[2]{0:T(128)S(1)} %pad_add_fusion.refs_0_, bf16[144,960]{1,0:T(8,128)(2,1)S(1)} %get-tuple-element.78.refs_1_, ...), custom_call_target="tpu_custom_call" | custom-call | flops 1 | bytes 1 | tf_op jit(solution)/shard_map/signal_stage/pallas_call | solution.py:297
  25.6 0.0 collective-permute-done.2.refs_2_
  25.6 3.5 %signal_stage.4 = (bf16[528,1920]{1,0:T(8,128)(2,1)S(1)}, f32[512,960]{1,0:T(8,128)S(1)}, f32[4,16,8,960]{3,2,1,0:T(8,128)S(1)}, f32[16,8,960]{2,1,0:T(8,128)S(1)}, f32[2,16,960]{2,1,0:T(8,128)S(1)}) custom-call(s32[2]{0:T(128)S(1)} %pad_add_fusion.refs_0_, ...), custom_call_target="tpu_custom_call", output_to_operand_aliasing={{0}: (3, {}), {1}: (4, {}), {2}: (5, {})} | custom-call | flops 1 | bytes 1 | tf_op jit(solution)/shard_map/signal_stage/pallas_call | solution.py:297
  29.1 1.8 %collective-permute-done.1.refs_2_ = bf16[128,960]{1,0:T(8,128)(2,1)S(1)} collective-permute-done((bf16[128,960]{1,0:T(8,128)(2,1)S(1)}, bf16[128,960]{1,0:T(8,128)(2,1)S(1)}, u32[]{:S(2)}, u32[]{:S(2)}) %collective-permute-start.1) | collective-permute-done | bytes 245792 | tf_op jit(solution)/shard_map/ppermute | solution.py:409
  30.9 4.3 %signal_stage.5 = (bf16[528,1920]{1,0:T(8,128)(2,1)S(1)}, f32[512,960]{1,0:T(8,128)S(1)}, f32[4,16,8,960]{3,2,1,0:T(8,128)S(1)}, f32[16,8,960]{2,1,0:T(8,128)S(1...) custom-call(s32[2]{0:T(128)S(1)} %pad_add_fusion.refs_0_, ...), custom_call_target="tpu_custom_call", output_to_operand_aliasing={{0}: (3, {}), {1}: (4, {}), {2}: (5, {})} | custom-call | flops 1 | bytes 1 | tf_op jit(solution)/shard_map/signal_stage/pallas_call | solution.py:297
  35.2 1.1 %collective-permute-start.5 = (f32[16,960]{1,0:T(8,128)S(1)}, f32[16,960]{1,0:T(8,128)S(1)}, u32[]{:S(2)}, u32[]{:S(2)}) collective-permute-start(f32[16,960]{1,0:T(8,128)S(1)} %get-tuple-element.101.refs_2_), channel_id=1, source_target_pairs={{6,0},{0,2},{2,4},{4,6},{14,8},{8,10},{10,12},{12,14},{22,16},{16,... | collective-permute-start | bytes 184328 | tf_op jit(solution)/shard_map/ppermute | solution.py:453
  36.3 2.2 %collective-permute-start.6 = (f32[16,960]{1,0:T(8,128)S(1)}, f32[16,960]{1,0:T(8,128)S(1)}, u32[]{:S(2)}, u32[]{:S(2)}) collective-permute-start(f32[16,960]{1,0:T(8,128)S(1)} %get-tuple-element.101.refs_2_), channel_id=1, source_target_pairs={{4,0},{6,2},{0,4},{2,6},{12,8},{14,10},{8,12},{10,14},{20,16},{22,... | collective-permute-start | bytes 184328 | tf_op jit(solution)/shard_map/ppermute | solution.py:453
  38.5 1.0 %collective-permute-start.7 = (f32[16,960]{1,0:T(8,128)S(1)}, f32[16,960]{1,0:T(8,128)S(1)}, u32[]{:S(2)}, u32[]{:S(2)}) collective-permute-start(f32[16,960]{1,0:T(8,128)S(1)} %get-tuple-element.101.refs_2_), channel_id=1, source_target_pairs={{2,0},{4,2},{6,4},{0,6},{10,8},{12,10},{14,12},{8,14},{18,16},{20,... | collective-permute-start | bytes 184328 | tf_op jit(solution)/shard_map/ppermute | solution.py:453
  39.5 1.7 %local_stage.3 = (f32[128,960]{1,0:T(8,128)S(1)}, f32[128,960]{1,0:T(8,128)S(1)}, f32[16,8,960]{2,1,0:T(8,128)S(1)}) custom-call(bf16[528,1920]{1,0:T(8,128)(2,1)S(1)} %get-tuple-element.123.refs_0_, f32[512,960]{1,0:T(8,128)S(1)} %get-tuple-element.124.refs_1_, f32[16,8,960]{2,1,0:T(8,128)S(1)} %get-tuple-element.102.refs_2_, ...), custom_call_target="tpu_custom_call" | custom-call | flops 1 | bytes 1 | tf_op jit(solution)/shard_map/local_stage/pallas_call | solution.py:297
  41.2 0.0 collective-permute-done.5.refs_3_
  41.2 0.0 collective-permute-done.6.refs_4_
  41.2 0.2 collective-permute-done.7.refs_5_
  41.4 0.6 combine_states.2
  42.0 4.0 %collective-permute-start.10 = (f32[16,960]{1,0:T(8,128)S(1)}, f32[16,960]{1,0:T(8,128)S(1)}, u32[]{:S(2)}, u32[]{:S(2)}) collective-permute-start(f32[16,960]{1,0:T(8,128)S(1)} %get-tuple-element.115.refs_2_), channel_id=1, source_target_pairs={{8,0},{10,2},{12,4},{14,6},{16,8},{18,10},{20,12},{22,14},{24,16},... | collective-permute-start | bytes 184328 | tf_op jit(solution)/shard_map/ppermute | solution.py:453
  46.0 0.0 collective-permute-start.8
  46.0 1.1 %collective-permute-start.9 = (f32[16,960]{1,0:T(8,128)S(1)}, f32[16,960]{1,0:T(8,128)S(1)}, u32[]{:S(2)}, u32[]{:S(2)}) collective-permute-start(f32[16,960]{1,0:T(8,128)S(1)} %get-tuple-element.115.refs_2_), channel_id=1, source_target_pairs={{16,0},{18,2},{20,4},{22,6},{24,8},{26,10},{28,12},{30,14},{0,16},... | collective-permute-start | bytes 184328 | tf_op jit(solution)/shard_map/ppermute | solution.py:453
  47.1 4.0 %local_stage.4 = (f32[256,960]{1,0:T(8,128)S(1)}, f32[256,960]{1,0:T(8,128)S(1)}) custom-call(bf16[528,1920]{1,0:T(8,128)(2,1)S(1)} %get-tuple-element.123.refs_0_, f32[512,960]{1,0:T(8,128)S(1)} %get-tuple-element.124.refs_1_, f32[16,8,960]{2,1,0:T(8,128)S(1)} %get-tuple-element.102.refs_2_, bf16[3,1920,960]{2,1,0:T(8,128)(2,1)S(1)} %load_weights.1.refs_6_.refs_9_.refs_3_, ...), custom_call_target="tpu_custom_call" | custom-call | flops 1 | bytes 1 | tf_op jit(solution)/shard_map/local_stage/pallas_call | solution.py:297
  51.1 0.0 collective-permute-done.10.refs_5_
  51.1 1.7 %collective-permute-done.8.refs_3_ = f32[16,960]{1,0:T(8,128)S(1)} collective-permute-done((f32[16,960]{1,0:T(8,128)S(1)}, f32[16,960]{1,0:T(8,128)S(1)}, u32[]{:S(2)}, u32[]{:S(2)}) %collective-permute-start.8) | collective-permute-done | bytes 61472 | tf_op jit(solution)/shard_map/ppermute | solution.py:453
  52.8 1.2 %collective-permute-done.9.refs_4_ = f32[16,960]{1,0:T(8,128)S(1)} collective-permute-done((f32[16,960]{1,0:T(8,128)S(1)}, f32[16,960]{1,0:T(8,128)S(1)}, u32[]{:S(2)}, u32[]{:S(2)}) %collective-permute-start.9) | collective-permute-done | bytes 61472 | tf_op jit(solution)/shard_map/ppermute | solution.py:453
  54.0 0.6 combine_states.3.refs_5_
  54.6 2.3 %second_stage.3 = (bf16[128,960]{1,0:T(8,128)(2,1)S(1)}, f32[128,960]{1,0:T(8,128)S(1)}) custom-call(s32[2]{0:T(128)S(1)} %pad_add_fusion.refs_0_, f32[128,960]{1,0:T(8,128)S(1)} %get-tuple-element.108.refs_1_, f32[128,960]{1,0:T(8,128)S(1)} %get-tuple-element.109.refs_2_, f32[16,8,960]{2,1,0:T(8,128)S(1)} %get-tuple-element.110.refs_3_, ...), custom_call_target="tpu_custom_call" | custom-call | flops 1 | bytes 1 | tf_op jit(solution)/shard_map/second_stage/pallas_call | solution.py:297
  56.9 1.6 %collective-permute-start.11 = (bf16[128,960]{1,0:T(8,128)(2,1)S(1)}, bf16[128,960]{1,0:T(8,128)(2,1)S(1)}, u32[]{:S(2)}, u32[]{:S(2)}) collective-permute-start(bf16[128,960]{1,0:T(8,128)(2,1)S(1)} %get-tuple-element.122), channel_id=1, source_target_pairs={{1,0},{0,1},{3,2},{2,3},{5,4},{4,5},{7,6},{6,7},{9,8},{8,9},{11,10... | collective-permute-start | bytes 737288 | tf_op jit(solution)/shard_map/ppermute | solution.py:409
  58.5 4.0 %second_stage.5 = (bf16[256,960]{1,0:T(8,128)(2,1)S(1)}, f32[256,960]{1,0:T(8,128)S(1)}) custom-call(s32[2]{0:T(128)S(1)} %pad_add_fusion.refs_0_, f32[256,960]{1,0:T(8,128)S(1)} %get-tuple-element.130.refs_1_, f32[256,960]{1,0:T(8,128)S(1)} %get-tuple-element.131.refs_2_, f32[16,8,960]{2,1,0:T(8,128)S(1)} %get-tuple-element.110.refs_3_, ...), custom_call_target="tpu_custom_call" | custom-call | flops 1 | bytes 1 | tf_op jit(solution)/shard_map/second_stage/pallas_call | solution.py:297
  62.5 0.6 collective-permute-start.13
  63.0 1.6 %collective-permute-done.11.refs_2_ = bf16[128,960]{1,0:T(8,128)(2,1)S(1)} collective-permute-done((bf16[128,960]{1,0:T(8,128)(2,1)S(1)}, bf16[128,960]{1,0:T(8,128)(2,1)S(1)}, u32[]{:S(2)}, u32[]{:S(2)}) %collective-permute-start.11) | collective-permute-done | bytes 245792 | tf_op jit(solution)/shard_map/ppermute | solution.py:409
  64.6 1.3 %local_stage.5 = (f32[128,960]{1,0:T(8,128)S(1)}, f32[128,960]{1,0:T(8,128)S(1)}) custom-call(bf16[528,1920]{1,0:T(8,128)(2,1)S(1)} %get-tuple-element.123.refs_0_, f32[512,960]{1,0:T(8,128)S(1)} %get-tuple-element.124.refs_1_, f32[16,8,960]{2,1,0:T(8,128)S(1)} %get-tuple-element.102.refs_2_, bf16[3,1920,960]{2,1,0:T(8,128)(2,1)S(1)} %load_weights.1.refs_6_.refs_9_.refs_3_, ...), custom_call_target="tpu_custom_call" | custom-call | flops 1 | bytes 1 | tf_op jit(solution)/shard_map/local_stage/pallas_call | solution.py:297
  65.9 2.4 %second_stage.4 = (bf16[128,960]{1,0:T(8,128)(2,1)S(1)}, f32[128,960]{1,0:T(8,128)S(1)}) custom-call(s32[2]{0:T(128)S(1)} %pad_add_fusion.refs_0_, f32[128,960]{1,0:T(8,128)S(1)} %get-tuple-element.125.refs_1_, f32[128,960]{1,0:T(8,128)S(1)} %get-tuple-element.126.refs_2_, f32[16,8,960]{2,1,0:T(8,128)S(1)} %get-tuple-element.110.refs_3_, ...), custom_call_target="tpu_custom_call" | custom-call | flops 1 | bytes 1 | tf_op jit(solution)/shard_map/second_stage/pallas_call | solution.py:297
  68.4 2.6 %collective-permute-start.12 = (bf16[128,960]{1,0:T(8,128)(2,1)S(1)}, bf16[128,960]{1,0:T(8,128)(2,1)S(1)}, u32[]{:S(2)}, u32[]{:S(2)}) collective-permute-start(bf16[128,960]{1,0:T(8,128)(2,1)S(1)} %get-tuple-element.128), channel_id=1, source_target_pairs={{1,0},{0,1},{3,2},{2,3},{5,4},{4,5},{7,6},{6,7},{9,8},{8,9},{11,10... | collective-permute-start | bytes 737288 | tf_op jit(solution)/shard_map/ppermute | solution.py:409
  70.9 6.4 %collective-permute-done.13.refs_3_ = bf16[256,960]{1,0:T(8,128)(2,1)S(1)} collective-permute-done((bf16[256,960]{1,0:T(8,128)(2,1)S(1)}, bf16[256,960]{1,0:T(8,128)(2,1)S(1)}, u32[]{:S(2)}, u32[]{:S(2)}) %collective-permute-start.13) | collective-permute-done | bytes 491552 | tf_op jit(solution)/shard_map/ppermute | solution.py:409
  77.4 0.8 last_stage.2.refs_2_
  78.1 2.1 %collective-permute-done.12.refs_1_ = bf16[128,960]{1,0:T(8,128)(2,1)S(1)} collective-permute-done((bf16[128,960]{1,0:T(8,128)(2,1)S(1)}, bf16[128,960]{1,0:T(8,128)(2,1)S(1)}, u32[]{:S(2)}, u32[]{:S(2)}) %collective-permute-start.12) | collective-permute-done | bytes 245792 | tf_op jit(solution)/shard_map/ppermute | solution.py:409
  80.2 1.4 %last_stage.3 = bf16[960,512]{1,0:T(8,128)(2,1)} custom-call(f32[128,960]{1,0:T(8,128)S(1)} %get-tuple-element.127.refs_0_, bf16[128,960]{1,0:T(8,128)(2,1)S(1)} %collective-permute-done.12.refs_1_, f32[960,512]{1,0:T(8,128)S(1)} %last_stage.2.refs_2_), custom_call_target="tpu_custom_call" | custom-call | flops 1 | bytes 1 | tf_op jit(solution)/shard_map/last_stage/pallas_call | solution.py:297
  (14 shorter events, 0.1 us)
Async XLA Ops:
  0.0 10.0 %copy-start.1 = (f32[16,960]{1,0:T(8,128)S(1)}, f32[16,960]{1,0:T(8,128)}, u32[]{:S(2)}) copy-start(f32[16,960]{1,0:T(8,128)} %refs_6_.5) | copy-start | bytes 184324
  0.1 1.2 %copy-start.2 = (bf16[960,512]{1,0:T(8,128)(2,1)S(1)}, bf16[960,512]{1,0:T(8,128)(2,1)}, u32[]{:S(2)}) copy-start(bf16[960,512]{1,0:T(8,128)(2,1)} %tokens_ref.1) | copy-start | bytes 2949124
  1.3 8.7 %copy-start.6 = (f32[1920]{0:T(1024)S(1)}, f32[1920]{0:T(1024)}, u32[]{:S(2)}) copy-start(f32[1920]{0:T(1024)} %param.9) | copy-start | bytes 23044
  1.3 8.7 %copy-start.5 = (f32[16,960]{1,0:T(8,128)S(1)}, f32[16,960]{1,0:T(8,128)}, u32[]{:S(2)}) copy-start(f32[16,960]{1,0:T(8,128)} %param.13) | copy-start | bytes 184324
  1.9 5.8 %collective-permute-start = (bf16[16,960]{1,0:T(8,128)(2,1)S(1)}, bf16[16,960]{1,0:T(8,128)(2,1)S(1)}, u32[]{:S(2)}, u32[]{:S(2)}) collective-permute-start(bf16[16,960]{1,0:T(8,128)(2,1)S(1)} %get-tuple-element.72), channel_id=1, source_target_pairs={{0,2},{2,4},{4,6},{6,8},{8,10},{10,12},{12,14},{14,16},{16,18},{18... | collective-permute-start | bytes 92168 | tf_op jit(solution)/shard_map/ppermute | solution.py:485
  4.3 11.1 %collective-permute-start.3 = (bf16[144,960]{1,0:T(8,128)(2,1)S(1)}, bf16[144,960]{1,0:T(8,128)(2,1)S(1)}, u32[]{:S(2)}, u32[]{:S(2)}) collective-permute-start(bf16[144,960]{1,0:T(8,128)(2,1)S(1)} %get-tuple-element.78.refs_1_), channel_id=1, source_target_pairs={{1,0},{0,1},{3,2},{2,3},{5,4},{4,5},{7,6},{6,7},{9,8},{8,9},{11,10... | collective-permute-start | bytes 829448 | tf_op jit(solution)/shard_map/ppermute | solution.py:409
  7.8 11.9 %collective-permute-start.4 = (bf16[144,960]{1,0:T(8,128)(2,1)S(1)}, bf16[144,960]{1,0:T(8,128)(2,1)S(1)}, u32[]{:S(2)}, u32[]{:S(2)}) collective-permute-start(bf16[144,960]{1,0:T(8,128)(2,1)S(1)} %join_edge.1.refs_3_), channel_id=1, source_target_pairs={{1,0},{0,1},{3,2},{2,3},{5,4},{4,5},{7,6},{6,7},{9,8},{8,9},{11,10... | collective-permute-start | bytes 829448 | tf_op jit(solution)/shard_map/ppermute | solution.py:409
  7.9 17.7 %collective-permute-start.2 = (bf16[128,960]{1,0:T(8,128)(2,1)S(1)}, bf16[128,960]{1,0:T(8,128)(2,1)S(1)}, u32[]{:S(2)}, u32[]{:S(2)}) collective-permute-start(bf16[128,960]{1,0:T(8,128)(2,1)S(1)} %get-tuple-element.77.refs_1_), channel_id=1, source_target_pairs={{1,0},{0,1},{3,2},{2,3},{5,4},{4,5},{7,6},{6,7},{9,8},{8,9},{11,10... | collective-permute-start | bytes 737288 | tf_op jit(solution)/shard_map/ppermute | solution.py:409
  9.9 21.0 %collective-permute-start.1 = (bf16[128,960]{1,0:T(8,128)(2,1)S(1)}, bf16[128,960]{1,0:T(8,128)(2,1)S(1)}, u32[]{:S(2)}, u32[]{:S(2)}) collective-permute-start(bf16[128,960]{1,0:T(8,128)(2,1)S(1)} %get-tuple-element.76.refs_1_), channel_id=1, source_target_pairs={{1,0},{0,1},{3,2},{2,3},{5,4},{4,5},{7,6},{6,7},{9,8},{8,9},{11,10... | collective-permute-start | bytes 737288 | tf_op jit(solution)/shard_map/ppermute | solution.py:409
  10.1 9.6 %copy-start.3 = (f32[3,3,960]{2,1,0:T(4,128)S(1)}, f32[3,3,960]{2,1,0:T(4,128)}, u32[]{:S(2)}) copy-start(f32[3,3,960]{2,1,0:T(4,128)} %refs_4_.5) | copy-start | bytes 103684
  30.9 8.6 %copy-start.4 = (f32[960]{0:T(1024)S(1)}, f32[960]{0:T(1024)}, u32[]{:S(2)}) copy-start(f32[960]{0:T(1024)} %param.14) | copy-start | bytes 11524
  35.2 5.9 %collective-permute-start.5 = (f32[16,960]{1,0:T(8,128)S(1)}, f32[16,960]{1,0:T(8,128)S(1)}, u32[]{:S(2)}, u32[]{:S(2)}) collective-permute-start(f32[16,960]{1,0:T(8,128)S(1)} %get-tuple-element.101.refs_2_), channel_id=1, source_target_pairs={{6,0},{0,2},{2,4},{4,6},{14,8},{8,10},{10,12},{12,14},{22,16},{16,... | collective-permute-start | bytes 184328 | tf_op jit(solution)/shard_map/ppermute | solution.py:453
  36.3 4.9 %collective-permute-start.6 = (f32[16,960]{1,0:T(8,128)S(1)}, f32[16,960]{1,0:T(8,128)S(1)}, u32[]{:S(2)}, u32[]{:S(2)}) collective-permute-start(f32[16,960]{1,0:T(8,128)S(1)} %get-tuple-element.101.refs_2_), channel_id=1, source_target_pairs={{4,0},{6,2},{0,4},{2,6},{12,8},{14,10},{8,12},{10,14},{20,16},{22,... | collective-permute-start | bytes 184328 | tf_op jit(solution)/shard_map/ppermute | solution.py:453
  38.5 2.9 %collective-permute-start.7 = (f32[16,960]{1,0:T(8,128)S(1)}, f32[16,960]{1,0:T(8,128)S(1)}, u32[]{:S(2)}, u32[]{:S(2)}) collective-permute-start(f32[16,960]{1,0:T(8,128)S(1)} %get-tuple-element.101.refs_2_), channel_id=1, source_target_pairs={{2,0},{4,2},{6,4},{0,6},{10,8},{12,10},{14,12},{8,14},{18,16},{20,... | collective-permute-start | bytes 184328 | tf_op jit(solution)/shard_map/ppermute | solution.py:453
  42.0 9.1 %collective-permute-start.10 = (f32[16,960]{1,0:T(8,128)S(1)}, f32[16,960]{1,0:T(8,128)S(1)}, u32[]{:S(2)}, u32[]{:S(2)}) collective-permute-start(f32[16,960]{1,0:T(8,128)S(1)} %get-tuple-element.115.refs_2_), channel_id=1, source_target_pairs={{8,0},{10,2},{12,4},{14,6},{16,8},{18,10},{20,12},{22,14},{24,16},... | collective-permute-start | bytes 184328 | tf_op jit(solution)/shard_map/ppermute | solution.py:453
  46.0 6.8 %collective-permute-start.8 = (f32[16,960]{1,0:T(8,128)S(1)}, f32[16,960]{1,0:T(8,128)S(1)}, u32[]{:S(2)}, u32[]{:S(2)}) collective-permute-start(f32[16,960]{1,0:T(8,128)S(1)} %get-tuple-element.115.refs_2_), channel_id=1, source_target_pairs={{24,0},{26,2},{28,4},{30,6},{0,8},{2,10},{4,12},{6,14},{8,16},{10,... | collective-permute-start | bytes 184328 | tf_op jit(solution)/shard_map/ppermute | solution.py:453
  46.0 8.0 %collective-permute-start.9 = (f32[16,960]{1,0:T(8,128)S(1)}, f32[16,960]{1,0:T(8,128)S(1)}, u32[]{:S(2)}, u32[]{:S(2)}) collective-permute-start(f32[16,960]{1,0:T(8,128)S(1)} %get-tuple-element.115.refs_2_), channel_id=1, source_target_pairs={{16,0},{18,2},{20,4},{22,6},{24,8},{26,10},{28,12},{30,14},{0,16},... | collective-permute-start | bytes 184328 | tf_op jit(solution)/shard_map/ppermute | solution.py:453
  47.1 7.5 %copy-start = (bf16[960,1920]{1,0:T(8,128)(2,1)S(1)}, bf16[960,1920]{1,0:T(8,128)(2,1)}, u32[]{:S(2)}) copy-start(bf16[960,1920]{1,0:T(8,128)(2,1)} %refs_8_.7) | copy-start | bytes 11059204
  56.9 7.8 %collective-permute-start.11 = (bf16[128,960]{1,0:T(8,128)(2,1)S(1)}, bf16[128,960]{1,0:T(8,128)(2,1)S(1)}, u32[]{:S(2)}, u32[]{:S(2)}) collective-permute-start(bf16[128,960]{1,0:T(8,128)(2,1)S(1)} %get-tuple-element.122), channel_id=1, source_target_pairs={{1,0},{0,1},{3,2},{2,3},{5,4},{4,5},{7,6},{6,7},{9,8},{8,9},{11,10... | collective-permute-start | bytes 737288 | tf_op jit(solution)/shard_map/ppermute | solution.py:409
  62.5 14.9 %collective-permute-start.13 = (bf16[256,960]{1,0:T(8,128)(2,1)S(1)}, bf16[256,960]{1,0:T(8,128)(2,1)S(1)}, u32[]{:S(2)}, u32[]{:S(2)}) collective-permute-start(bf16[256,960]{1,0:T(8,128)(2,1)S(1)} %get-tuple-element.134), channel_id=1, source_target_pairs={{1,0},{0,1},{3,2},{2,3},{5,4},{4,5},{7,6},{6,7},{9,8},{8,9},{11,10... | collective-permute-start | bytes 1474568 | tf_op jit(solution)/shard_map/ppermute | solution.py:409
  68.4 11.8 %collective-permute-start.12 = (bf16[128,960]{1,0:T(8,128)(2,1)S(1)}, bf16[128,960]{1,0:T(8,128)(2,1)S(1)}, u32[]{:S(2)}, u32[]{:S(2)}) collective-permute-start(bf16[128,960]{1,0:T(8,128)(2,1)S(1)} %get-tuple-element.128), channel_id=1, source_target_pairs={{1,0},{0,1},{3,2},{2,3},{5,4},{4,5},{7,6},{6,7},{9,8},{8,9},{11,10... | collective-permute-start | bytes 737288 | tf_op jit(solution)/shard_map/ppermute | solution.py:409
where the time goes:
time: 81.7 us; the launch traced here: 81.6 us
  Pallas kernels  39.8 us (49%)
  starting transfers between devices  21 us (26%)
  waiting for transfers between devices  19.2 us (24%)
  local copies, waits for them, and re-layouts  1.23 us (2%)
    pallas_call x16, Pallas kernels, call(): pl.pallas_call(kernel, out_shape=outs, in_specs=[smem] * len(scalars) + [...  34.5 us
    ppermute x7, waiting for transfers between devices, rotate(): lax.ppermute(value, axis, [((i + steps) % count, i) for i in range(count)])  16.2 us
    ppermute x7, starting transfers between devices, rotate(): lax.ppermute(value, axis, [((i + steps) % count, i) for i in range(count)])  9.3 us
    ppermute x6, starting transfers between devices, carried_in(): others.append(lax.ppermute(total, axis, pairs))  9.29 us
    pallas_call x1, Pallas kernels, in_vmem(): pl.pallas_call(functools.partial(load_weights, places), out_shape=pltpu.V...  5.29 us
    ppermute x6, waiting for transfers between devices, carried_in(): others.append(lax.ppermute(total, axis, pairs))  3.05 us
    ppermute x1, starting transfers between devices, body(): lax.ppermute(edge, 'ctx', [(i, i + 1) for i in range(lax.axis_size('ctx')...  2.37 us
  transfers between devices with their start and end apart: 14, of which 8 were waited for; matrix products, arithmetic and copies ran while one was open for 0% of the time, Pallas kernels for 37%

commit v1 on v0

--- a/solution.py
+++ b/solution.py
@@ -46,13 +46,26 @@
     return lax.dot_general(pick, tokens, CONTRACT_LAST, preferred_element_type=F32).astype(BF16)
 
 
-def first_rows(halo, tokens_ref, out_ref, edge_ref):
-    tokens = tokens_ref.shape[1]
-    out_ref[...] = turned(token_picker(-halo, out_ref.shape[0], tokens), tokens_ref[...])
+def first_rows(halo, tokens_hbm, out_ref, edge_ref, tokens_ref, sem):
+    share, tokens = tokens_ref.shape
+    parts = [slice(low, min(low + BLOCK, share)) for low in range(0, share, BLOCK)]
+    copies = [
+        pltpu.make_async_copy(tokens_hbm.at[part], tokens_ref.at[part], sem.at[k])
+        for k, part in enumerate(parts)
+    ]
+    for copy in copies:
+        copy.start()
+    pick = token_picker(-halo, out_ref.shape[0], tokens)
     row = lax.broadcasted_iota(jnp.int32, (halo, tokens), 0)
     column = lax.broadcasted_iota(jnp.int32, (halo, tokens), 1)
     wanted = jnp.where(lax.rem(row, ROWS) == 0, tokens - halo // ROWS + lax.div(row, ROWS), -1)
-    edge_ref[...] = turned(jnp.where(column == wanted, 1.0, 0.0).astype(BF16), tokens_ref[...])
+    pick = jnp.concatenate([pick, jnp.where(column == wanted, 1.0, 0.0).astype(BF16)], axis=0)
+    rows = out_ref.shape[0]
+    for part, copy in zip(parts, copies):
+        copy.wait()
+        picked = turned(pick, tokens_ref[part, :])
+        out_ref[:, part] = picked[:rows]
+        edge_ref[:, part] = picked[rows:]
 
 
 def next_rows(row, tokens_ref, *chunk_refs):
@@ -62,9 +75,10 @@
         row += ref.shape[0]
 
 
-def join_edge(edge_ref, chunk_ref, out_ref):
+def join_edge(place_ref, edge_ref, chunk_ref, out_ref):
     halo = edge_ref.shape[0]
-    out_ref[:halo, :] = edge_ref[...]
+    preceded = jnp.where(place_ref[1] > 0, 1.0, 0.0)
+    out_ref[:halo, :] = (edge_ref[...].astype(F32) * preceded).astype(BF16)
     out_ref[halo:, :] = chunk_ref[...]
 
 
@@ -103,7 +117,7 @@
         _, _, _, states_in, tail_in = [refs.pop(0) for _ in range(5)]
     gain_ref, w_ref, short_ref, rate_ref = refs[:4]
     normed_ref, signal_ref, marks_ref, states_ref, tail_ref = refs[4:9]
-    total_ref = refs[9] if last else None
+    total_ref, sent_ref = refs[9:11] if last else (None, None)
     x_ref, p_ref = refs[-2:]
     halo = ROWS * (taps - 1)
     modes, channels = rate_ref.shape
@@ -174,6 +188,7 @@
                     total_ref[n : n + 1, lanes] = jnp.sum(
                         states[n] * jnp.exp(-rate[n] * left), axis=0, keepdims=True
                     )
+                sent_ref[:, lanes] = total_ref[:, lanes].astype(BF16)
 
 
 def local_stage(row, rows, taps, *refs):
@@ -307,6 +322,26 @@
     )(*scalars, *operands)
 
 
+def run_first_rows(tokens, halo, size):
+    share = tokens.shape[0]
+    return pl.pallas_call(
+        functools.partial(first_rows, halo),
+        out_shape=[
+            jax.ShapeDtypeStruct((halo + size, share), BF16),
+            jax.ShapeDtypeStruct((halo, share), BF16),
+        ],
+        in_specs=[pl.BlockSpec(memory_space=pl.ANY)],
+        out_specs=[pl.BlockSpec(memory_space=pltpu.VMEM)] * 2,
+        scratch_shapes=[
+            pltpu.VMEM(tokens.shape, BF16),
+            pltpu.SemaphoreType.DMA((-(-share // BLOCK),)),
+        ],
+        compiler_params=pltpu.CompilerParams(vmem_limit_bytes=56 * 2**20),
+        cost_estimate=pl.CostEstimate(flops=1, bytes_accessed=1, transcendentals=0),
+        name="first_rows",
+    )(tokens)
+
+
 def in_vmem(w):
     streams, channels, features = w.shape
     block = min(BLOCK, channels)
@@ -344,7 +379,7 @@
         jax.ShapeDtypeStruct((streams - 1, halo, channels), F32),
     ]
     if last:
-        outs.append(jax.ShapeDtypeStruct((modes, channels), F32))
+        outs += [jax.ShapeDtypeStruct((modes, channels), kind) for kind in (F32, BF16)]
     inputs = 1 + len(tokens) * pieces
     return call(
         functools.partial(signal_stage, pieces, len(tokens), first, last, row, taps),
@@ -423,7 +458,8 @@
     before = jnp.zeros(rate.shape, F32)
     for shift in range(1, radix):
         reached = jnp.where(digit >= shift, 1.0, 0.0)
-        before = before + jnp.exp(-rate * (unit * (shift - 1))) * (others[shift - 1][...] * reached)
+        other = others[shift - 1][...].astype(F32)
+        before = before + jnp.exp(-rate * (unit * (shift - 1))) * (other * reached)
     if stride > 1:
         carry_ref[...] = carry_in[...] + jnp.exp(-rate * (span * inner).astype(F32)) * before
     else:
@@ -433,11 +469,12 @@
         for shift in range(1, radix):
             at = lax.rem(digit - shift + radix, radix)
             weight = jnp.exp(-rate * (unit * (radix - 1 - at)).astype(F32))
-            new = new + weight * others[shift - 1][...]
-        refs[-1][...] = new
-
-
-def carried_in(state, rate, span, axis, place, between):
+            new = new + weight * others[shift - 1][...].astype(F32)
+        refs[-2][...] = new
+        refs[-1][...] = new.astype(BF16)
+
+
+def carried_in(state, sent, rate, span, axis, place, between):
     count = lax.axis_size(axis)
     total, stride, carry = state, 1, []
     while stride < count:
@@ -450,19 +487,19 @@
             for i in range(count):
                 digit = (i // stride) % radix
                 pairs.append((i + ((digit - shift) % radix - digit) * stride, i))
-            others.append(lax.ppermute(total, axis, pairs))
-        others = between(others)
+            others.append(lax.ppermute(sent, axis, pairs))
+        others = between(stride, others)
         shape = jax.ShapeDtypeStruct(state.shape, F32)
         carry = call(
             functools.partial(combine_states, span, stride, radix, count),
             "combine_states",
             [place],
             [rate, total, *others, *carry],
-            [shape] * (2 if group < count else 1),
+            [shape, shape, jax.ShapeDtypeStruct(state.shape, BF16)] if group < count else [shape],
             [],
         )
         if group < count:
-            *carry, total = carry
+            *carry, total, sent = carry
         stride = group
     return carry[0]
 
@@ -478,16 +515,13 @@
 
     place = jnp.stack([lax.axis_index("tp"), lax.axis_index("ctx")]).astype(jnp.int32)
     tokens, place = lax.optimization_barrier((tokens, place))
-    x0, edge = call(
-        functools.partial(first_rows, halo), "first_rows", [], [tokens],
-        [bf16_rows(halo + sizes[0]), bf16_rows(halo)], [],
-    )
-    edge = lax.ppermute(edge, "ctx", [(i, i + 1) for i in range(lax.axis_size("ctx") - 1)])
+    x0, edge = run_first_rows(tokens, halo, sizes[0])
+    edge = rotate(edge, "ctx", -1)
     x1, *others = call(
         functools.partial(next_rows, sizes[0]), "next_rows", [], [tokens],
         [bf16_rows(size) for size in sizes[1:]], [],
     )
-    (x1,) = call(join_edge, "join_edge", [], [edge, x1], [bf16_rows(halo + sizes[1])], [])
+    (x1,) = call(join_edge, "join_edge", [place], [edge, x1], [bf16_rows(halo + sizes[1])], [])
     x1, others = lax.optimization_barrier((x1, others))
     x = [x0, x1, *others]
     residue, norm_gain, skip_gain, *_ = lax.optimization_barrier((residue, norm_gain, skip_gain, *x))
@@ -507,9 +541,11 @@
         before = results[:5]
         row += sum(sizes[j] for j in group)
     normed, signal, marks, states, _ = before
-    state, normed, signal, states = lax.optimization_barrier((results[5], normed, signal, states))
-    out_sizes = [rows // 4, rows // 2, rows // 4]
-    out_rows = [0, rows // 4, 3 * rows // 4]
+    state, sent, normed, signal, states = lax.optimization_barrier(
+        (results[5], results[6], normed, signal, states)
+    )
+    out_sizes = [rows // 4] * 4
+    out_rows = [sum(out_sizes[:j]) for j in range(4)]
     small = [w_in, w_short, decay_rate, mode, skip]
     done = []
 
@@ -517,22 +553,24 @@
         k = len(done)
         done.append(run_local(out_rows[k], out_sizes[k], taps, normed, signal, states, *small))
 
-    def between(others):
-        if len(done) < 2:
+    def between(stride, others):
+        if stride > 1 and not done:
             local_part()
             others, done[-1] = lax.optimization_barrier((others, done[-1]))
         return others
 
-    carry = carried_in(state, decay_rate, rows, "ctx", place, between)
-    while len(done) < 2:
+    carry = carried_in(state, sent, decay_rate, rows, "ctx", place, between)
+    if not done:
         local_part()
     begin = done[0][2]
     own, came = [], []
     for j in range(len(out_sizes)):
-        if j == 2:
-            normed, signal, came[: pieces - 1] = lax.optimization_barrier(
-                (normed, signal, came[: pieces - 1])
+        if j >= 2:
+            arrived = slice((j - 2) * (pieces - 1), (j - 1) * (pieces - 1))
+            normed, signal, carry, came[arrived] = lax.optimization_barrier(
+                (normed, signal, carry, came[arrived])
             )
+        if j > 0:
             local_part()
         send, kept = run_second(
             pieces, out_rows[j], out_sizes[j], rows, place, *done[j][:2], begin, marks, carry,

time: 81.7 us -> 79.9 us (0.978)
  waiting for transfers between devices: 19.2 us -> 15.1 us
  Pallas kernels: 39.8 us -> 42.3 us
    ppermute x7 -> x9, waiting for transfers between devices: 16.2 us -> 10.3 us  [rotate(): lax.ppermute(value, axis, [((i + steps) % count, i) for i in range(count)])]
    ppermute x7 -> x6, starting transfers between devices: 11.7 us -> 7.57 us  [carried_in(): others.append(lax.ppermute(sent, axis, pairs))]
    ppermute x7 -> x9, starting transfers between devices: 9.3 us -> 13.2 us  [rotate(): lax.ppermute(value, axis, [((i + steps) % count, i) for i in range(count)])]
    pallas_call x0 -> x1, Pallas kernels: none -> 2.84 us  [run_first_rows(): pl.pallas_call(functools.partial(first_rows, halo), out_shape=[jax.ShapeD...]
    ppermute x7 -> x6, waiting for transfers between devices: 3.05 us -> 4.74 us  [carried_in(): others.append(lax.ppermute(sent, axis, pairs))]
    pallas_call x16 -> x17, Pallas kernels: 34.5 us -> 34.2 us  [call(): pl.pallas_call(kernel, out_shape=outs, in_specs=[smem] * len(scalars) + [...]
  transfers between devices with their start and end apart: 14 -> 15, of which waited for: 8 -> 9; matrix products, arithmetic and copies ran while one was open for 0% -> 0% of each run, Pallas kernels for 37% -> 38%
where the time goes in v1:
time: 79.9 us; the launch traced here: 79.7 us
  Pallas kernels  42.3 us (53%)
  starting transfers between devices  20.7 us (26%)
  waiting for transfers between devices  15.1 us (19%)
  local copies, waits for them, and re-layouts  1.24 us (2%)
    pallas_call x17, Pallas kernels, call(): pl.pallas_call(kernel, out_shape=outs, in_specs=[smem] * len(scalars) + [...  34.2 us
    ppermute x9, starting transfers between devices, rotate(): lax.ppermute(value, axis, [((i + steps) % count, i) for i in range(count)])  13.2 us
    ppermute x9, waiting for transfers between devices, rotate(): lax.ppermute(value, axis, [((i + steps) % count, i) for i in range(count)])  10.3 us
    ppermute x6, starting transfers between devices, carried_in(): others.append(lax.ppermute(sent, axis, pairs))  7.57 us
    pallas_call x1, Pallas kernels, in_vmem(): pl.pallas_call(functools.partial(load_weights, places), out_shape=pltpu.V...  5.33 us
    ppermute x6, waiting for transfers between devices, carried_in(): others.append(lax.ppermute(sent, axis, pairs))  4.74 us
    pallas_call x1, Pallas kernels, run_first_rows(): pl.pallas_call(functools.partial(first_rows, halo), out_shape=[jax.ShapeD...  2.84 us
  transfers between devices with their start and end apart: 15, of which 9 were waited for; matrix products, arithmetic and copies ran while one was open for 0% of the time, Pallas kernels for 38%

profile of v1, /device:TPU:0, one launch (start us, length us, event | category | flops | bytes accessed | tf_op | source)
XLA Modules:
  0.0 79.7 jit_solution(8602884320362682875)
XLA Ops:
  0.0 0.1 pad_add_fusion.place_ref.refs_0_
  0.1 2.8 %first_rows.1 = (bf16[144,960]{1,0:T(8,128)(2,1)}, bf16[16,960]{1,0:T(8,128)(2,1)}) custom-call(bf16[960,512]{1,0:T(8,128)(2,1)} %tokens_ref), custom_call_target="tpu_custom_call" | custom-call | flops 1 | bytes 1 | tf_op jit(solution)/shard_map/first_rows/pallas_call | solution.py:327
  2.9 0.5 collective-permute-start
  3.4 2.6 %collective-permute-start.3 = (bf16[144,960]{1,0:T(8,128)(2,1)}, bf16[144,960]{1,0:T(8,128)(2,1)S(1)}, u32[]{:S(2)}, u32[]{:S(2)}) collective-permute-start(bf16[144,960]{1,0:T(8,128)(2,1)} %get-tuple-element.85.refs_1_), channel_id=1, source_target_pairs={{1,0},{0,1},{3,2},{2,3},{5,4},{4,5},{7,6},{6,7},{9,8},{8,9},{11,10... | collective-permute-start | bytes 829448 | tf_op jit(solution)/shard_map/ppermute | solution.py:444
  6.0 1.2 %copy-done.2 = bf16[960,512]{1,0:T(8,128)(2,1)S(1)} copy-done((bf16[960,512]{1,0:T(8,128)(2,1)S(1)}, bf16[960,512]{1,0:T(8,128)(2,1)}, u32[]{:S(2)}) %copy-start.2) | copy-done | bytes 983064
  7.2 1.0 %next_rows.1 = (bf16[128,960]{1,0:T(8,128)(2,1)S(1)}, bf16[128,960]{1,0:T(8,128)(2,1)S(1)}, bf16[128,960]{1,0:T(8,128)(2,1)S(1)}) custom-call(bf16[960,512]{1,0:T(8,128)(2,1)S(1)} %copy-done.2), custom_call_target="tpu_custom_call" | custom-call | flops 1 | bytes 1 | tf_op jit(solution)/shard_map/next_rows/pallas_call | solution.py:312
  8.3 1.9 %collective-permute-done.edge_ref = bf16[16,960]{1,0:T(8,128)(2,1)S(1)} collective-permute-done((bf16[16,960]{1,0:T(8,128)(2,1)}, bf16[16,960]{1,0:T(8,128)(2,1)S(1)}, u32[]{:S(2)}, u32[]{:S(2)}) %collective-permute-start) | collective-permute-done | bytes 30752 | tf_op jit(solution)/shard_map/ppermute | solution.py:444
  10.2 0.6 join_edge.1.refs_3_
  10.8 2.1 %collective-permute-start.4 = (bf16[144,960]{1,0:T(8,128)(2,1)S(1)}, bf16[144,960]{1,0:T(8,128)(2,1)S(1)}, u32[]{:S(2)}, u32[]{:S(2)}) collective-permute-start(bf16[144,960]{1,0:T(8,128)(2,1)S(1)} %join_edge.1.refs_3_), channel_id=1, source_target_pairs={{1,0},{0,1},{3,2},{2,3},{5,4},{4,5},{7,6},{6,7},{9,8},{8,9},{11,10... | collective-permute-start | bytes 829448 | tf_op jit(solution)/shard_map/ppermute | solution.py:444
  12.8 0.1 collective-permute-start.2
  12.9 1.9 %collective-permute-start.1 = (bf16[128,960]{1,0:T(8,128)(2,1)S(1)}, bf16[128,960]{1,0:T(8,128)(2,1)S(1)}, u32[]{:S(2)}, u32[]{:S(2)}) collective-permute-start(bf16[128,960]{1,0:T(8,128)(2,1)S(1)} %get-tuple-element.83.refs_1_), channel_id=1, source_target_pairs={{1,0},{0,1},{3,2},{2,3},{5,4},{4,5},{7,6},{6,7},{9,8},{8,9},{11,10... | collective-permute-start | bytes 737288 | tf_op jit(solution)/shard_map/ppermute | solution.py:444
  15.0 0.0 copy-start.3
  15.0 0.0 copy-start.4
  15.0 5.3 %load_weights.1.refs_6_.refs_9_.refs_3_ = bf16[3,1920,960]{2,1,0:T(8,128)(2,1)S(1)} custom-call(bf16[3,960,1920]{2,1,0:T(8,128)(2,1)} %w_hbm), custom_call_target="tpu_custom_call" | custom-call | flops 1 | bytes 1 | tf_op jit(solution)/shard_map/load_weights/pallas_call | solution.py:353
  20.3 0.0 collective-permute-done.3.refs_2_
  20.3 0.5 collective-permute-done.4.refs_4_
  20.8 5.9 %signal_stage.3 = (bf16[528,1920]{1,0:T(8,128)(2,1)S(1)}, f32[512,960]{1,0:T(8,128)S(1)}, f32[4,16,8,960]{3,2,1,0:T(8,128)S(1)}, f32[16,8,960]{2,1,0:T(8,128)S(1)}, f32[2,16,960]{2,1,0:T(8,128)S(1)}) custom-call(s32[2]{0:T(128)S(1)} %pad_add_fusion.place_ref.refs_0_, bf16[144,960]{1,0:T(8,128)(2,1)S(1)} %copy-done.4, ...), custom_call_target="tpu_custom_call" | custom-call | flops 1 | bytes 1 | tf_op jit(solution)/shard_map/signal_stage/pallas_call | solution.py:312
  26.7 0.0 collective-permute-done.2.refs_2_
  26.7 3.5 %signal_stage.4 = (bf16[528,1920]{1,0:T(8,128)(2,1)S(1)}, f32[512,960]{1,0:T(8,128)S(1)}, f32[4,16,8,960]{3,2,1,0:T(8,128)S(1)}, f32[16,8,960]{2,1,0:T(8,128)S(1)}, f32[2,16,960]{2,1,0:T(8,128)S(1)}) custom-call(s32[2]{0:T(128)S(1)} %pad_add_fusion.place_ref.refs_0_, ...), custom_call_target="tpu_custom_call", output_to_operand_aliasing={{0}: (3, {}), {1}: (4, {}), {2}: (5, {})} | custom-call | flops 1 | bytes 1 | tf_op jit(solution)/shard_map/signal_stage/pallas_call | solution.py:312
  30.3 1.4 %collective-permute-done.1.refs_2_ = bf16[128,960]{1,0:T(8,128)(2,1)S(1)} collective-permute-done((bf16[128,960]{1,0:T(8,128)(2,1)S(1)}, bf16[128,960]{1,0:T(8,128)(2,1)S(1)}, u32[]{:S(2)}, u32[]{:S(2)}) %collective-permute-start.1) | collective-permute-done | bytes 245792 | tf_op jit(solution)/shard_map/ppermute | solution.py:444
  31.7 4.4 %signal_stage.5 = (bf16[528,1920]{1,0:T(8,128)(2,1)S(1)}, f32[512,960]{1,0:T(8,128)S(1)}, f32[4,16,8,960]{3,2,1,0:T(8,128)S(1)}, f32[16,8,960]{2,1,0:T(8,128)S(1...) custom-call(s32[2]{0:T(128)S(1)} %pad_add_fusion.place_ref.refs_0_, ...), custom_call_target="tpu_custom_call", output_to_operand_aliasing={{0}: (3, {}), {1}: (4, {}), {2}: (5, {})} | custom-call | flops 1 | bytes 1 | tf_op jit(solution)/shard_map/signal_stage/pallas_call | solution.py:312
  36.0 1.8 %collective-permute-start.6 = (bf16[16,960]{1,0:T(8,128)(2,1)S(1)}, bf16[16,960]{1,0:T(8,128)(2,1)S(1)}, u32[]{:S(2)}, u32[]{:S(2)}) collective-permute-start(bf16[16,960]{1,0:T(8,128)(2,1)S(1)} %get-tuple-element.110), channel_id=1, source_target_pairs={{4,0},{6,2},{0,4},{2,6},{12,8},{14,10},{8,12},{10,14},{20,16},{22,... | collective-permute-start | bytes 92168 | tf_op jit(solution)/shard_map/ppermute | solution.py:490
  37.8 1.1 %collective-permute-start.7 = (bf16[16,960]{1,0:T(8,128)(2,1)S(1)}, bf16[16,960]{1,0:T(8,128)(2,1)S(1)}, u32[]{:S(2)}, u32[]{:S(2)}) collective-permute-start(bf16[16,960]{1,0:T(8,128)(2,1)S(1)} %get-tuple-element.110), channel_id=1, source_target_pairs={{2,0},{4,2},{6,4},{0,6},{10,8},{12,10},{14,12},{8,14},{18,16},{20,... | collective-permute-start | bytes 92168 | tf_op jit(solution)/shard_map/ppermute | solution.py:490
  38.9 0.5 collective-permute-done.5.refs_3_
  39.4 0.6 collective-permute-done.6.refs_4_
  40.0 0.5 collective-permute-done.7.refs_5_
  40.5 0.6 combine_states.2
  41.2 3.6 %collective-permute-start.10 = (bf16[16,960]{1,0:T(8,128)(2,1)S(1)}, bf16[16,960]{1,0:T(8,128)(2,1)S(1)}, u32[]{:S(2)}, u32[]{:S(2)}) collective-permute-start(bf16[16,960]{1,0:T(8,128)(2,1)S(1)} %get-tuple-element.112), channel_id=1, source_target_pairs={{8,0},{10,2},{12,4},{14,6},{16,8},{18,10},{20,12},{22,14},{24,16},... | collective-permute-start | bytes 92168 | tf_op jit(solution)/shard_map/ppermute | solution.py:490
  44.8 1.1 %collective-permute-start.9 = (bf16[16,960]{1,0:T(8,128)(2,1)S(1)}, bf16[16,960]{1,0:T(8,128)(2,1)S(1)}, u32[]{:S(2)}, u32[]{:S(2)}) collective-permute-start(bf16[16,960]{1,0:T(8,128)(2,1)S(1)} %get-tuple-element.112), channel_id=1, source_target_pairs={{16,0},{18,2},{20,4},{22,6},{24,8},{26,10},{28,12},{30,14},{0,16},... | collective-permute-start | bytes 92168 | tf_op jit(solution)/shard_map/ppermute | solution.py:490
  45.8 1.7 %local_stage.4 = (f32[128,960]{1,0:T(8,128)S(1)}, f32[128,960]{1,0:T(8,128)S(1)}, f32[16,8,960]{2,1,0:T(8,128)S(1)}) custom-call(bf16[528,1920]{1,0:T(8,128)(2,1)S(1)} %get-tuple-element.134.refs_0_, f32[512,960]{1,0:T(8,128)S(1)} %get-tuple-element.135.refs_1_, f32[16,8,960]{2,1,0:T(8,128)S(1)} %get-tuple-element.113.refs_2_, ...), custom_call_target="tpu_custom_call" | custom-call | flops 1 | bytes 1 | tf_op jit(solution)/shard_map/local_stage/pallas_call | solution.py:312
  47.5 3.1 %collective-permute-done.8.refs_3_ = bf16[16,960]{1,0:T(8,128)(2,1)S(1)} collective-permute-done((bf16[16,960]{1,0:T(8,128)(2,1)S(1)}, bf16[16,960]{1,0:T(8,128)(2,1)S(1)}, u32[]{:S(2)}, u32[]{:S(2)}) %collective-permute-start.8) | collective-permute-done | bytes 30752 | tf_op jit(solution)/shard_map/ppermute | solution.py:490
  50.7 0.6 combine_states.3.refs_5_
  51.3 2.5 %second_stage.4 = (bf16[128,960]{1,0:T(8,128)(2,1)S(1)}, f32[128,960]{1,0:T(8,128)S(1)}) custom-call(s32[2]{0:T(128)S(1)} %pad_add_fusion.place_ref.refs_0_, f32[128,960]{1,0:T(8,128)S(1)} %get-tuple-element.123.refs_1_, f32[128,960]{1,0:T(8,128)S(1)} %get-tuple-element.124.refs_2_, f32[16,8,960]{2,1,0:T(8,128)S(1)} %get-tuple-element.125.refs_3_, ...), custom_call_target="tpu_custom_call" | custom-call | flops 1 | bytes 1 | tf_op jit(solution)/shard_map/second_stage/pallas_call | solution.py:312
  53.8 1.6 %collective-permute-start.11 = (bf16[128,960]{1,0:T(8,128)(2,1)S(1)}, bf16[128,960]{1,0:T(8,128)(2,1)S(1)}, u32[]{:S(2)}, u32[]{:S(2)}) collective-permute-start(bf16[128,960]{1,0:T(8,128)(2,1)S(1)} %get-tuple-element.127), channel_id=1, source_target_pairs={{1,0},{0,1},{3,2},{2,3},{5,4},{4,5},{7,6},{6,7},{9,8},{8,9},{11,10... | collective-permute-start | bytes 737288 | tf_op jit(solution)/shard_map/ppermute | solution.py:444
  55.4 1.3 %local_stage.5 = (f32[128,960]{1,0:T(8,128)S(1)}, f32[128,960]{1,0:T(8,128)S(1)}) custom-call(bf16[528,1920]{1,0:T(8,128)(2,1)S(1)} %get-tuple-element.134.refs_0_, f32[512,960]{1,0:T(8,128)S(1)} %get-tuple-element.135.refs_1_, f32[16,8,960]{2,1,0:T(8,128)S(1)} %get-tuple-element.113.refs_2_, bf16[3,1920,960]{2,1,0:T(8,128)(2,1)S(1)} %load_weights.1.refs_6_.refs_9_.refs_3_, ...), custom_call_target="tpu_custom_call" | custom-call | flops 1 | bytes 1 | tf_op jit(solution)/shard_map/local_stage/pallas_call | solution.py:312
  56.8 2.4 %second_stage.5 = (bf16[128,960]{1,0:T(8,128)(2,1)S(1)}, f32[128,960]{1,0:T(8,128)S(1)}) custom-call(s32[2]{0:T(128)S(1)} %pad_add_fusion.place_ref.refs_0_, f32[128,960]{1,0:T(8,128)S(1)} %get-tuple-element.131.refs_1_, f32[128,960]{1,0:T(8,128)S(1)} %get-tuple-element.132.refs_2_, f32[16,8,960]{2,1,0:T(8,128)S(1)} %get-tuple-element.125.refs_3_, ...), custom_call_target="tpu_custom_call" | custom-call | flops 1 | bytes 1 | tf_op jit(solution)/shard_map/second_stage/pallas_call | solution.py:312
  59.2 0.5 collective-permute-start.12
  59.7 2.1 %collective-permute-done.11.refs_3_ = bf16[128,960]{1,0:T(8,128)(2,1)S(1)} collective-permute-done((bf16[128,960]{1,0:T(8,128)(2,1)S(1)}, bf16[128,960]{1,0:T(8,128)(2,1)S(1)}, u32[]{:S(2)}, u32[]{:S(2)}) %collective-permute-start.11) | collective-permute-done | bytes 245792 | tf_op jit(solution)/shard_map/ppermute | solution.py:444
  61.8 1.3 %local_stage.7 = (f32[128,960]{1,0:T(8,128)S(1)}, f32[128,960]{1,0:T(8,128)S(1)}) custom-call(bf16[528,1920]{1,0:T(8,128)(2,1)S(1)} %get-tuple-element.134.refs_0_, f32[512,960]{1,0:T(8,128)S(1)} %get-tuple-element.135.refs_1_, f32[16,8,960]{2,1,0:T(8,128)S(1)} %get-tuple-element.113.refs_2_, bf16[3,1920,960]{2,1,0:T(8,128)(2,1)S(1)} %load_weights.1.refs_6_.refs_9_.refs_3_, ...), custom_call_target="tpu_custom_call" | custom-call | flops 1 | bytes 1 | tf_op jit(solution)/shard_map/local_stage/pallas_call | solution.py:312
  63.2 2.4 %second_stage.7 = (bf16[128,960]{1,0:T(8,128)(2,1)S(1)}, f32[128,960]{1,0:T(8,128)S(1)}) custom-call(s32[2]{0:T(128)S(1)} %pad_add_fusion.place_ref.refs_0_, f32[128,960]{1,0:T(8,128)S(1)} %get-tuple-element.143.refs_1_, f32[128,960]{1,0:T(8,128)S(1)} %get-tuple-element.144.refs_2_, f32[16,8,960]{2,1,0:T(8,128)S(1)} %get-tuple-element.125.refs_3_, ...), custom_call_target="tpu_custom_call" | custom-call | flops 1 | bytes 1 | tf_op jit(solution)/shard_map/second_stage/pallas_call | solution.py:312
  65.6 2.5 %collective-permute-start.14 = (bf16[128,960]{1,0:T(8,128)(2,1)S(1)}, bf16[128,960]{1,0:T(8,128)(2,1)S(1)}, u32[]{:S(2)}, u32[]{:S(2)}) collective-permute-start(bf16[128,960]{1,0:T(8,128)(2,1)S(1)} %get-tuple-element.148), channel_id=1, source_target_pairs={{1,0},{0,1},{3,2},{2,3},{5,4},{4,5},{7,6},{6,7},{9,8},{8,9},{11,10... | collective-permute-start | bytes 737288 | tf_op jit(solution)/shard_map/ppermute | solution.py:444
  68.1 1.3 %local_stage.6 = (f32[128,960]{1,0:T(8,128)S(1)}, f32[128,960]{1,0:T(8,128)S(1)}) custom-call(bf16[528,1920]{1,0:T(8,128)(2,1)S(1)} %get-tuple-element.134.refs_0_, f32[512,960]{1,0:T(8,128)S(1)} %get-tuple-element.135.refs_1_, f32[16,8,960]{2,1,0:T(8,128)S(1)} %get-tuple-element.113.refs_2_, bf16[3,1920,960]{2,1,0:T(8,128)(2,1)S(1)} %load_weights.1.refs_6_.refs_9_.refs_3_, ...), custom_call_target="tpu_custom_call" | custom-call | flops 1 | bytes 1 | tf_op jit(solution)/shard_map/local_stage/pallas_call | solution.py:312
  69.4 2.4 %second_stage.6 = (bf16[128,960]{1,0:T(8,128)(2,1)S(1)}, f32[128,960]{1,0:T(8,128)S(1)}) custom-call(s32[2]{0:T(128)S(1)} %pad_add_fusion.place_ref.refs_0_, f32[128,960]{1,0:T(8,128)S(1)} %get-tuple-element.136.refs_1_, f32[128,960]{1,0:T(8,128)S(1)} %get-tuple-element.137.refs_2_, f32[16,8,960]{2,1,0:T(8,128)S(1)} %get-tuple-element.125.refs_3_, ...), custom_call_target="tpu_custom_call" | custom-call | flops 1 | bytes 1 | tf_op jit(solution)/shard_map/second_stage/pallas_call | solution.py:312
  71.9 1.3 %collective-permute-start.13 = (bf16[128,960]{1,0:T(8,128)(2,1)S(1)}, bf16[128,960]{1,0:T(8,128)(2,1)S(1)}, u32[]{:S(2)}, u32[]{:S(2)}) collective-permute-start(bf16[128,960]{1,0:T(8,128)(2,1)S(1)} %get-tuple-element.140), channel_id=1, source_target_pairs={{1,0},{0,1},{3,2},{2,3},{5,4},{4,5},{7,6},{6,7},{9,8},{8,9},{11,10... | collective-permute-start | bytes 737288 | tf_op jit(solution)/shard_map/ppermute | solution.py:444
  73.2 0.0 collective-permute-done.14.refs_5_
  73.2 0.7 last_stage.2.refs_2_
  73.9 4.4 %collective-permute-done.13.refs_1_ = bf16[128,960]{1,0:T(8,128)(2,1)S(1)} collective-permute-done((bf16[128,960]{1,0:T(8,128)(2,1)S(1)}, bf16[128,960]{1,0:T(8,128)(2,1)S(1)}, u32[]{:S(2)}, u32[]{:S(2)}) %collective-permute-start.13) | collective-permute-done | bytes 245792 | tf_op jit(solution)/shard_map/ppermute | solution.py:444
  78.3 1.4 %last_stage.3 = bf16[960,512]{1,0:T(8,128)(2,1)} custom-call(f32[128,960]{1,0:T(8,128)S(1)} %get-tuple-element.139.refs_0_, bf16[128,960]{1,0:T(8,128)(2,1)S(1)} %collective-permute-done.13.refs_1_, f32[960,512]{1,0:T(8,128)S(1)} %last_stage.2.refs_2_), custom_call_target="tpu_custom_call" | custom-call | flops 1 | bytes 1 | tf_op jit(solution)/shard_map/last_stage/pallas_call | solution.py:312
  (20 shorter events, 0.1 us)
Async XLA Ops:
  0.0 14.9 %copy-start.6 = (f32[16,960]{1,0:T(8,128)S(1)}, f32[16,960]{1,0:T(8,128)}, u32[]{:S(2)}) copy-start(f32[16,960]{1,0:T(8,128)} %param.13) | copy-start | bytes 184324
  0.0 14.9 %copy-start.7 = (f32[1920]{0:T(1024)S(1)}, f32[1920]{0:T(1024)}, u32[]{:S(2)}) copy-start(f32[1920]{0:T(1024)} %param.9) | copy-start | bytes 23044
  0.0 14.9 %copy-start.1 = (f32[16,960]{1,0:T(8,128)S(1)}, f32[16,960]{1,0:T(8,128)}, u32[]{:S(2)}) copy-start(f32[16,960]{1,0:T(8,128)} %refs_6_.7) | copy-start | bytes 184324
  2.9 7.3 %collective-permute-start = (bf16[16,960]{1,0:T(8,128)(2,1)}, bf16[16,960]{1,0:T(8,128)(2,1)S(1)}, u32[]{:S(2)}, u32[]{:S(2)}) collective-permute-start(bf16[16,960]{1,0:T(8,128)(2,1)} %get-tuple-element.79), channel_id=1, source_target_pairs={{30,0},{0,2},{2,4},{4,6},{6,8},{8,10},{10,12},{12,14},{14,16},{16,... | collective-permute-start | bytes 92168 | tf_op jit(solution)/shard_map/ppermute | solution.py:444
  3.4 16.9 %collective-permute-start.3 = (bf16[144,960]{1,0:T(8,128)(2,1)}, bf16[144,960]{1,0:T(8,128)(2,1)S(1)}, u32[]{:S(2)}, u32[]{:S(2)}) collective-permute-start(bf16[144,960]{1,0:T(8,128)(2,1)} %get-tuple-element.85.refs_1_), channel_id=1, source_target_pairs={{1,0},{0,1},{3,2},{2,3},{5,4},{4,5},{7,6},{6,7},{9,8},{8,9},{11,10... | collective-permute-start | bytes 829448 | tf_op jit(solution)/shard_map/ppermute | solution.py:444
  6.0 1.2 %copy-start.2 = (bf16[960,512]{1,0:T(8,128)(2,1)S(1)}, bf16[960,512]{1,0:T(8,128)(2,1)}, u32[]{:S(2)}) copy-start(bf16[960,512]{1,0:T(8,128)(2,1)} %tokens_ref) | copy-start | bytes 2949124
  10.8 10.0 %collective-permute-start.4 = (bf16[144,960]{1,0:T(8,128)(2,1)S(1)}, bf16[144,960]{1,0:T(8,128)(2,1)S(1)}, u32[]{:S(2)}, u32[]{:S(2)}) collective-permute-start(bf16[144,960]{1,0:T(8,128)(2,1)S(1)} %join_edge.1.refs_3_), channel_id=1, source_target_pairs={{1,0},{0,1},{3,2},{2,3},{5,4},{4,5},{7,6},{6,7},{9,8},{8,9},{11,10... | collective-permute-start | bytes 829448 | tf_op jit(solution)/shard_map/ppermute | solution.py:444
  12.8 13.9 %collective-permute-start.2 = (bf16[128,960]{1,0:T(8,128)(2,1)S(1)}, bf16[128,960]{1,0:T(8,128)(2,1)S(1)}, u32[]{:S(2)}, u32[]{:S(2)}) collective-permute-start(bf16[128,960]{1,0:T(8,128)(2,1)S(1)} %get-tuple-element.84.refs_1_), channel_id=1, source_target_pairs={{1,0},{0,1},{3,2},{2,3},{5,4},{4,5},{7,6},{6,7},{9,8},{8,9},{11,10... | collective-permute-start | bytes 737288 | tf_op jit(solution)/shard_map/ppermute | solution.py:444
  12.9 18.7 %collective-permute-start.1 = (bf16[128,960]{1,0:T(8,128)(2,1)S(1)}, bf16[128,960]{1,0:T(8,128)(2,1)S(1)}, u32[]{:S(2)}, u32[]{:S(2)}) collective-permute-start(bf16[128,960]{1,0:T(8,128)(2,1)S(1)} %get-tuple-element.83.refs_1_), channel_id=1, source_target_pairs={{1,0},{0,1},{3,2},{2,3},{5,4},{4,5},{7,6},{6,7},{9,8},{8,9},{11,10... | collective-permute-start | bytes 737288 | tf_op jit(solution)/shard_map/ppermute | solution.py:444
  15.0 5.8 %copy-start.3 = (f32[3,3,960]{2,1,0:T(4,128)S(1)}, f32[3,3,960]{2,1,0:T(4,128)}, u32[]{:S(2)}) copy-start(f32[3,3,960]{2,1,0:T(4,128)} %refs_4_.7) | copy-start | bytes 103684
  15.0 5.8 %copy-start.4 = (bf16[144,960]{1,0:T(8,128)(2,1)S(1)}, bf16[144,960]{1,0:T(8,128)(2,1)}, u32[]{:S(2)}) copy-start(bf16[144,960]{1,0:T(8,128)(2,1)} %get-tuple-element.85.refs_1_) | copy-start | bytes 829444
  31.7 14.2 %copy-start.5 = (f32[960]{0:T(1024)S(1)}, f32[960]{0:T(1024)}, u32[]{:S(2)}) copy-start(f32[960]{0:T(1024)} %param.14) | copy-start | bytes 11524
  36.0 3.3 %collective-permute-start.5 = (bf16[16,960]{1,0:T(8,128)(2,1)S(1)}, bf16[16,960]{1,0:T(8,128)(2,1)S(1)}, u32[]{:S(2)}, u32[]{:S(2)}) collective-permute-start(bf16[16,960]{1,0:T(8,128)(2,1)S(1)} %get-tuple-element.110), channel_id=1, source_target_pairs={{6,0},{0,2},{2,4},{4,6},{14,8},{8,10},{10,12},{12,14},{22,16},{16,... | collective-permute-start | bytes 92168 | tf_op jit(solution)/shard_map/ppermute | solution.py:490
  36.0 3.9 %collective-permute-start.6 = (bf16[16,960]{1,0:T(8,128)(2,1)S(1)}, bf16[16,960]{1,0:T(8,128)(2,1)S(1)}, u32[]{:S(2)}, u32[]{:S(2)}) collective-permute-start(bf16[16,960]{1,0:T(8,128)(2,1)S(1)} %get-tuple-element.110), channel_id=1, source_target_pairs={{4,0},{6,2},{0,4},{2,6},{12,8},{14,10},{8,12},{10,14},{20,16},{22,... | collective-permute-start | bytes 92168 | tf_op jit(solution)/shard_map/ppermute | solution.py:490
  37.8 2.7 %collective-permute-start.7 = (bf16[16,960]{1,0:T(8,128)(2,1)S(1)}, bf16[16,960]{1,0:T(8,128)(2,1)S(1)}, u32[]{:S(2)}, u32[]{:S(2)}) collective-permute-start(bf16[16,960]{1,0:T(8,128)(2,1)S(1)} %get-tuple-element.110), channel_id=1, source_target_pairs={{2,0},{4,2},{6,4},{0,6},{10,8},{12,10},{14,12},{8,14},{18,16},{20,... | collective-permute-start | bytes 92168 | tf_op jit(solution)/shard_map/ppermute | solution.py:490
  41.2 6.4 %collective-permute-start.10 = (bf16[16,960]{1,0:T(8,128)(2,1)S(1)}, bf16[16,960]{1,0:T(8,128)(2,1)S(1)}, u32[]{:S(2)}, u32[]{:S(2)}) collective-permute-start(bf16[16,960]{1,0:T(8,128)(2,1)S(1)} %get-tuple-element.112), channel_id=1, source_target_pairs={{8,0},{10,2},{12,4},{14,6},{16,8},{18,10},{20,12},{22,14},{24,16},... | collective-permute-start | bytes 92168 | tf_op jit(solution)/shard_map/ppermute | solution.py:490
  44.8 5.9 %collective-permute-start.8 = (bf16[16,960]{1,0:T(8,128)(2,1)S(1)}, bf16[16,960]{1,0:T(8,128)(2,1)S(1)}, u32[]{:S(2)}, u32[]{:S(2)}) collective-permute-start(bf16[16,960]{1,0:T(8,128)(2,1)S(1)} %get-tuple-element.112), channel_id=1, source_target_pairs={{24,0},{26,2},{28,4},{30,6},{0,8},{2,10},{4,12},{6,14},{8,16},{10,... | collective-permute-start | bytes 92168 | tf_op jit(solution)/shard_map/ppermute | solution.py:490
  44.8 5.9 %collective-permute-start.9 = (bf16[16,960]{1,0:T(8,128)(2,1)S(1)}, bf16[16,960]{1,0:T(8,128)(2,1)S(1)}, u32[]{:S(2)}, u32[]{:S(2)}) collective-permute-start(bf16[16,960]{1,0:T(8,128)(2,1)S(1)} %get-tuple-element.112), channel_id=1, source_target_pairs={{16,0},{18,2},{20,4},{22,6},{24,8},{26,10},{28,12},{30,14},{0,16},... | collective-permute-start | bytes 92168 | tf_op jit(solution)/shard_map/ppermute | solution.py:490
  45.8 5.5 %copy-start = (bf16[960,1920]{1,0:T(8,128)(2,1)S(1)}, bf16[960,1920]{1,0:T(8,128)(2,1)}, u32[]{:S(2)}) copy-start(bf16[960,1920]{1,0:T(8,128)(2,1)} %refs_8_.9) | copy-start | bytes 11059204
  53.8 8.0 %collective-permute-start.11 = (bf16[128,960]{1,0:T(8,128)(2,1)S(1)}, bf16[128,960]{1,0:T(8,128)(2,1)S(1)}, u32[]{:S(2)}, u32[]{:S(2)}) collective-permute-start(bf16[128,960]{1,0:T(8,128)(2,1)S(1)} %get-tuple-element.127), channel_id=1, source_target_pairs={{1,0},{0,1},{3,2},{2,3},{5,4},{4,5},{7,6},{6,7},{9,8},{8,9},{11,10... | collective-permute-start | bytes 737288 | tf_op jit(solution)/shard_map/ppermute | solution.py:444
  59.2 8.9 %collective-permute-start.12 = (bf16[128,960]{1,0:T(8,128)(2,1)S(1)}, bf16[128,960]{1,0:T(8,128)(2,1)S(1)}, u32[]{:S(2)}, u32[]{:S(2)}) collective-permute-start(bf16[128,960]{1,0:T(8,128)(2,1)S(1)} %get-tuple-element.133), channel_id=1, source_target_pairs={{1,0},{0,1},{3,2},{2,3},{5,4},{4,5},{7,6},{6,7},{9,8},{8,9},{11,10... | collective-permute-start | bytes 737288 | tf_op jit(solution)/shard_map/ppermute | solution.py:444
  65.6 7.6 %collective-permute-start.14 = (bf16[128,960]{1,0:T(8,128)(2,1)S(1)}, bf16[128,960]{1,0:T(8,128)(2,1)S(1)}, u32[]{:S(2)}, u32[]{:S(2)}) collective-permute-start(bf16[128,960]{1,0:T(8,128)(2,1)S(1)} %get-tuple-element.148), channel_id=1, source_target_pairs={{1,0},{0,1},{3,2},{2,3},{5,4},{4,5},{7,6},{6,7},{9,8},{8,9},{11,10... | collective-permute-start | bytes 737288 | tf_op jit(solution)/shard_map/ppermute | solution.py:444
  71.9 6.4 %collective-permute-start.13 = (bf16[128,960]{1,0:T(8,128)(2,1)S(1)}, bf16[128,960]{1,0:T(8,128)(2,1)S(1)}, u32[]{:S(2)}, u32[]{:S(2)}) collective-permute-start(bf16[128,960]{1,0:T(8,128)(2,1)S(1)} %get-tuple-element.140), channel_id=1, source_target_pairs={{1,0},{0,1},{3,2},{2,3},{5,4},{4,5},{7,6},{6,7},{9,8},{8,9},{11,10... | collective-permute-start | bytes 737288 | tf_op jit(solution)/shard_map/ppermute | solution.py:444

commit v2 on v1

--- a/solution.py
+++ b/solution.py
@@ -46,40 +46,25 @@
     return lax.dot_general(pick, tokens, CONTRACT_LAST, preferred_element_type=F32).astype(BF16)
 
 
-def first_rows(halo, tokens_hbm, out_ref, edge_ref, tokens_ref, sem):
-    share, tokens = tokens_ref.shape
-    parts = [slice(low, min(low + BLOCK, share)) for low in range(0, share, BLOCK)]
-    copies = [
-        pltpu.make_async_copy(tokens_hbm.at[part], tokens_ref.at[part], sem.at[k])
-        for k, part in enumerate(parts)
-    ]
-    for copy in copies:
-        copy.start()
-    pick = token_picker(-halo, out_ref.shape[0], tokens)
+def first_rows(halo, size, tokens_ref, out_ref, edge_ref):
+    tokens = tokens_ref.shape[1]
     row = lax.broadcasted_iota(jnp.int32, (halo, tokens), 0)
     column = lax.broadcasted_iota(jnp.int32, (halo, tokens), 1)
     wanted = jnp.where(lax.rem(row, ROWS) == 0, tokens - halo // ROWS + lax.div(row, ROWS), -1)
-    pick = jnp.concatenate([pick, jnp.where(column == wanted, 1.0, 0.0).astype(BF16)], axis=0)
-    rows = out_ref.shape[0]
-    for part, copy in zip(parts, copies):
-        copy.wait()
-        picked = turned(pick, tokens_ref[part, :])
-        out_ref[:, part] = picked[:rows]
-        edge_ref[:, part] = picked[rows:]
-
-
-def next_rows(row, tokens_ref, *chunk_refs):
+    picks = [
+        token_picker(-halo, halo, tokens),
+        token_picker(size - halo, halo + size, tokens),
+        jnp.where(column == wanted, 1.0, 0.0).astype(BF16),
+    ]
+    rows = turned(jnp.concatenate(picks, axis=0), tokens_ref[...])
+    out_ref[...] = rows[: 2 * halo + size]
+    edge_ref[...] = rows[2 * halo + size :]
+
+
+def next_rows(firsts, tokens_ref, *chunk_refs):
     tokens = tokens_ref.shape[1]
-    for ref in chunk_refs:
+    for row, ref in zip(firsts, chunk_refs):
         ref[...] = turned(token_picker(row, ref.shape[0], tokens), tokens_ref[...])
-        row += ref.shape[0]
-
-
-def join_edge(place_ref, edge_ref, chunk_ref, out_ref):
-    halo = edge_ref.shape[0]
-    preceded = jnp.where(place_ref[1] > 0, 1.0, 0.0)
-    out_ref[:halo, :] = (edge_ref[...].astype(F32) * preceded).astype(BF16)
-    out_ref[halo:, :] = chunk_ref[...]
 
 
 def load_weights(places, w_hbm, out_ref, w_ref, sem):
@@ -109,30 +94,36 @@
     return product.astype(BF16).astype(F32)
 
 
-def signal_stage(pieces, chunks, first, last, row, taps, *refs):
+def signal_stage(pieces, row, taps, *refs):
     refs = list(refs)
     me_ref = refs.pop(0)
-    token_refs = [[refs.pop(0) for _ in range(pieces)] for _ in range(chunks)]
-    if not first:
+    token_refs = [refs.pop(0) for _ in range(pieces)]
+    x_ref, p_ref = refs[-2:]
+    halo = ROWS * (taps - 1)
+    rows, share = p_ref.shape[0] - halo, token_refs[0].shape[1]
+    last, start = row == 0, row == rows
+    fresh = last or start
+    read = rows + halo if fresh else rows
+    halo_refs = [refs.pop(0) for _ in range(pieces)] if last else []
+    edge_refs = [refs.pop(0) for _ in range(pieces)] if last else []
+    if not start:
         _, _, _, states_in, tail_in = [refs.pop(0) for _ in range(5)]
     gain_ref, w_ref, short_ref, rate_ref = refs[:4]
     normed_ref, signal_ref, marks_ref, states_ref, tail_ref = refs[4:9]
     total_ref, sent_ref = refs[9:11] if last else (None, None)
-    x_ref, p_ref = refs[-2:]
-    halo = ROWS * (taps - 1)
     modes, channels = rate_ref.shape
-    read, share = x_ref.shape[0], token_refs[0][0].shape[1]
-    rows = read - halo if first else read
     length = signal_ref.shape[0] // ROWS
     me = me_ref[0]
 
-    values = []
-    for s in range(pieces):
-        value = [refs_of[s][...].astype(F32) for refs_of in token_refs]
-        if first:
-            front, edge = value[0][:halo], value[-1][:halo]
-            value = [front + edge, value[0][halo:], *value[1:-1], value[-1][halo:]]
-        values.append(jnp.concatenate(value, axis=0) if len(value) > 1 else value[0])
+    values = [ref[halo if start else 0 :, :].astype(F32) for ref in token_refs]
+    if last:
+        preceded = jnp.where(me_ref[1] > 0, 1.0, 0.0)
+        values = [
+            jnp.concatenate(
+                [near[:halo, :].astype(F32) + edge[...].astype(F32) * preceded, value], axis=0
+            )
+            for near, edge, value in zip(halo_refs, edge_refs, values)
+        ]
     for rank in range(pieces):
         chosen = values[0]
         for s in range(1, pieces):
@@ -141,14 +132,14 @@
     features = x_ref[...]
     mean = jnp.mean(features * features, axis=1, keepdims=True)
     normed = (features * lax.rsqrt(mean + 1e-06) * gain_ref[...]).astype(BF16)
-    begin = 0 if first else halo + row
+    begin = row if fresh else halo + row
     normed_ref[begin : begin + read, :] = normed
 
     for low in range(0, channels, BLOCK):
         width = min(BLOCK, channels - low)
         part = slice(low, low + width)
         for s in (1, 2):
-            if not first:
+            if not fresh:
                 p_ref[:halo, :width] = tail_in[s - 1, :, part]
             p_ref[halo + rows - read :, :width] = project(
                 normed_ref[begin : begin + read, :], w_ref, s, part
@@ -164,21 +155,27 @@
             rate = [rows_as(rate_ref[n : n + 1, lanes], size) for n in range(modes)]
             decay = [jnp.exp(-r) for r in rate]
 
-            if first:
+            if fresh:
                 states = (jnp.zeros((ROWS, size), F32),) * modes
             else:
                 states = tuple(states_in[n, :, lanes] for n in range(modes))
-            for at in range(row, row + rows, SPAN * ROWS):
-                mark = at // (SPAN * ROWS)
                 for n in range(modes):
-                    marks_ref[mark, n, :, lanes] = states[n]
-
-                def step(i, states):
-                    here = pl.ds(pl.multiple_of(at + i * ROWS, ROWS), ROWS)
-                    now = signal_ref[here, lanes]
-                    return tuple(states[n] * decay[n] + now for n in range(modes))
-
-                states = lax.fori_loop(0, SPAN, step, states, unroll=8)
+                    marks_ref[row // rows, n, :, lanes] = states[n]
+
+            def step(i, states):
+                here = pl.ds(pl.multiple_of(row + i * ROWS, ROWS), ROWS)
+                now = signal_ref[here, lanes]
+                return tuple(states[n] * decay[n] + now for n in range(modes))
+
+            states = lax.fori_loop(0, rows // ROWS, step, states, unroll=8)
+            if last:
+                later = length - rows // ROWS
+                for n in range(modes):
+                    marks_ref[1, n, :, lanes] = states[n]
+                states = tuple(
+                    states_in[n, :, lanes] + jnp.exp(-rate[n] * later) * states[n]
+                    for n in range(modes)
+                )
             for n in range(modes):
                 states_ref[n, :, lanes] = states[n]
             if last:
@@ -261,7 +258,11 @@
                     n : n + 1, lanes
                 ]
                 if mark > 0:
-                    state = marks_ref[mark, n, :, lanes] + state * jnp.exp(-rate[n] * (SPAN * mark))
+                    state = marks_ref[1, n, :, lanes] + state * jnp.exp(-rate[n] * SPAN)
+                if mark > 1:
+                    state = marks_ref[mark, n, :, lanes] + state * jnp.exp(
+                        -rate[n] * (SPAN * (mark - 1))
+                    )
                 states.append(mode_ref[n : n + 1, lanes] * state)
 
             def step(i, states):
@@ -320,26 +321,6 @@
         cost_estimate=pl.CostEstimate(flops=1, bytes_accessed=1, transcendentals=0),
         name=name,
     )(*scalars, *operands)
-
-
-def run_first_rows(tokens, halo, size):
-    share = tokens.shape[0]
-    return pl.pallas_call(
-        functools.partial(first_rows, halo),
-        out_shape=[
-            jax.ShapeDtypeStruct((halo + size, share), BF16),
-            jax.ShapeDtypeStruct((halo, share), BF16),
-        ],
-        in_specs=[pl.BlockSpec(memory_space=pl.ANY)],
-        out_specs=[pl.BlockSpec(memory_space=pltpu.VMEM)] * 2,
-        scratch_shapes=[
-            pltpu.VMEM(tokens.shape, BF16),
-            pltpu.SemaphoreType.DMA((-(-share // BLOCK),)),
-        ],
-        compiler_params=pltpu.CompilerParams(vmem_limit_bytes=56 * 2**20),
-        cost_estimate=pl.CostEstimate(flops=1, bytes_accessed=1, transcendentals=0),
-        name="first_rows",
-    )(tokens)
 
 
 def in_vmem(w):
@@ -365,33 +346,30 @@
     )(w)
 
 
-def run_signal(pieces, row, count, first, last, taps, place, tokens, before, gain, w_in, w_short, rate):
+def run_signal(pieces, row, rows, count, taps, place, tokens, edges, before, gain, w_in, w_short, rate):
     streams, features, channels = w_in.shape
     modes = rate.shape[0]
     halo = ROWS * (taps - 1)
-    read = sum(chunk[0].shape[0] for chunk in tokens) - (halo if first else 0)
-    rows = read - halo if first else read
     outs = [
         jax.ShapeDtypeStruct((halo + count, features), BF16),
         jax.ShapeDtypeStruct((count, channels), F32),
-        jax.ShapeDtypeStruct((count // (SPAN * ROWS), modes, ROWS, channels), F32),
+        jax.ShapeDtypeStruct((count // rows, modes, ROWS, channels), F32),
         jax.ShapeDtypeStruct((modes, ROWS, channels), F32),
         jax.ShapeDtypeStruct((streams - 1, halo, channels), F32),
     ]
-    if last:
+    if row == 0:
         outs += [jax.ShapeDtypeStruct((modes, channels), kind) for kind in (F32, BF16)]
-    inputs = 1 + len(tokens) * pieces
     return call(
-        functools.partial(signal_stage, pieces, len(tokens), first, last, row, taps),
+        functools.partial(signal_stage, pieces, row, taps),
         "signal_stage",
         [place],
-        [part for chunk in tokens for part in chunk] + list(before) + [gain, w_in, w_short, rate],
+        list(tokens) + list(edges) + list(before) + [gain, w_in, w_short, rate],
         outs,
         [
-            pltpu.VMEM((read, features), F32),
+            pltpu.VMEM((rows + (halo if row in (0, rows) else 0), features), F32),
             pltpu.VMEM((halo + rows, min(BLOCK, channels)), F32),
         ],
-        aliases={} if first else {inputs + k: k for k in range(3)},
+        aliases={1 + len(tokens) + len(edges) + k: k for k in range(3)} if before else {},
     )
 
 
@@ -510,36 +488,40 @@
     channels = w_in.shape[1]
     taps = w_short.shape[0]
     halo = ROWS * (taps - 1)
-    sizes = [rows // CHUNKS] * CHUNKS
+    size = SPAN * ROWS
+    assert rows == CHUNKS * size
     bf16_rows = lambda size: jax.ShapeDtypeStruct((size, share), BF16)
 
     place = jnp.stack([lax.axis_index("tp"), lax.axis_index("ctx")]).astype(jnp.int32)
     tokens, place = lax.optimization_barrier((tokens, place))
-    x0, edge = run_first_rows(tokens, halo, sizes[0])
+    x1, edge = call(
+        functools.partial(first_rows, halo, size), "first_rows", [], [tokens],
+        [bf16_rows(2 * halo + size), bf16_rows(halo)], [],
+    )
     edge = rotate(edge, "ctx", -1)
-    x1, *others = call(
-        functools.partial(next_rows, sizes[0]), "next_rows", [], [tokens],
-        [bf16_rows(size) for size in sizes[1:]], [],
-    )
-    (x1,) = call(join_edge, "join_edge", [place], [edge, x1], [bf16_rows(halo + sizes[1])], [])
-    x1, others = lax.optimization_barrier((x1, others))
-    x = [x0, x1, *others]
+    tokens, x1 = lax.optimization_barrier((tokens, x1))
+    x0, *others = call(
+        functools.partial(next_rows, [0] + [j * size for j in range(2, CHUNKS)]), "next_rows",
+        [], [tokens], [bf16_rows(size)] * (CHUNKS - 1), [],
+    )
+    x = [x1, *others, x0]
     residue, norm_gain, skip_gain, *_ = lax.optimization_barrier((residue, norm_gain, skip_gain, *x))
     mode = residue * jnp.sqrt(-jnp.expm1(-2.0 * decay_rate))
     gain = norm_gain[None, :]
     skip = skip_gain[None, :]
-    parts = [[part] + [rotate(part, "tp", s) for s in range(1, pieces)] for part in x]
     w_in, mode, gain, skip, *_ = lax.optimization_barrier((w_in, mode, gain, skip, *x))
-    w_in = pltpu.with_memory_space_constraint(in_vmem(w_in), pltpu.VMEM)
-
-    before, row = [], 0
-    for group in [[0, 1]] + [[j] for j in range(2, CHUNKS)]:
+    w_in = in_vmem(w_in)
+    edge, w_in = lax.optimization_barrier((edge, w_in))
+    w_in = pltpu.with_memory_space_constraint(w_in, pltpu.VMEM)
+    *parts, edges = [[part] + [rotate(part, "tp", s) for s in range(1, pieces)] for part in x + [edge]]
+
+    before = []
+    for part, j in zip(parts, list(range(1, CHUNKS)) + [0]):
         results = run_signal(
-            pieces, row, rows, group[0] == 0, group[-1] == CHUNKS - 1, taps, place,
-            [parts[j] for j in group], before, gain, w_in, w_short, decay_rate,
+            pieces, j * size, size, rows, taps, place, part, [] if j else parts[0] + edges, before, gain, w_in,
+            w_short, decay_rate,
         )
         before = results[:5]
-        row += sum(sizes[j] for j in group)
     normed, signal, marks, states, _ = before
     state, sent, normed, signal, states = lax.optimization_barrier(
         (results[5], results[6], normed, signal, states)

time: 79.9 us -> 78.9 us (0.987)
  Pallas kernels: 42.3 us -> 41.1 us
  waiting for transfers between devices: 15.1 us -> 14 us
  other arithmetic: 0.12 us -> 0.99 us
    pallas_call x1 -> x0, Pallas kernels: 2.84 us -> none  [run_first_rows(): pl.pallas_call(functools.partial(first_rows, halo), out_shape=[jax.ShapeD...]
    pallas_call x17 -> x18, Pallas kernels: 34.2 us -> 35.8 us  [call(): pl.pallas_call(kernel, out_shape=outs, in_specs=[smem] * len(scalars) + [...]
    ppermute x9 -> x10, waiting for transfers between devices: 10.3 us -> 9.08 us  [rotate(): lax.ppermute(value, axis, [((i + steps) % count, i) for i in range(count)])]
    mul x1, other arithmetic: 0.05 us -> 0.92 us  [body(): mode = residue * jnp.sqrt(-jnp.expm1(-2.0 * decay_rate))]
    ppermute x9 -> x10, starting transfers between devices: 13.2 us -> 13.3 us  [rotate(): lax.ppermute(value, axis, [((i + steps) % count, i) for i in range(count)])]
  transfers between devices with their start and end apart: 15 -> 16, of which waited for: 9 -> 9; matrix products, arithmetic and copies ran while one was open for 0% -> 1% of each run, Pallas kernels for 38% -> 39%
where the time goes in v2:
time: 78.9 us; the launch traced here: 78.7 us
  Pallas kernels  41.1 us (52%)
  starting transfers between devices  21.2 us (27%)
  waiting for transfers between devices  14 us (18%)
  local copies, waits for them, and re-layouts  1.23 us (2%)
  other arithmetic  0.99 us (1%)
    pallas_call x18, Pallas kernels, call(): pl.pallas_call(kernel, out_shape=outs, in_specs=[smem] * len(scalars) + [...  35.8 us
    ppermute x10, starting transfers between devices, rotate(): lax.ppermute(value, axis, [((i + steps) % count, i) for i in range(count)])  13.3 us
    ppermute x10, waiting for transfers between devices, rotate(): lax.ppermute(value, axis, [((i + steps) % count, i) for i in range(count)])  9.08 us
    ppermute x6, starting transfers between devices, carried_in(): others.append(lax.ppermute(sent, axis, pairs))  7.87 us
    pallas_call x1, Pallas kernels, in_vmem(): pl.pallas_call(functools.partial(load_weights, places), out_shape=pltpu.V...  5.31 us
    ppermute x6, waiting for transfers between devices, carried_in(): others.append(lax.ppermute(sent, axis, pairs))  4.92 us
  transfers between devices with their start and end apart: 16, of which 9 were waited for; matrix products, arithmetic and copies ran while one was open for 1% of the time, Pallas kernels for 39%

profile of v2, /device:TPU:0, one launch (start us, length us, event | category | flops | bytes accessed | tf_op | source)
XLA Modules:
  0.0 78.7 jit_solution(7517116157298033901)
XLA Ops:
  0.0 0.1 pad_add_fusion.refs_0_
  0.1 1.2 %copy-done.2 = bf16[960,512]{1,0:T(8,128)(2,1)S(1)} copy-done((bf16[960,512]{1,0:T(8,128)(2,1)S(1)}, bf16[960,512]{1,0:T(8,128)(2,1)}, u32[]{:S(2)}) %copy-start.2) | copy-done | bytes 983064
  1.3 0.5 first_rows.1
  1.8 3.0 %collective-permute-start.1 = (bf16[160,960]{1,0:T(8,128)(2,1)S(1)}, bf16[160,960]{1,0:T(8,128)(2,1)S(1)}, u32[]{:S(2)}, u32[]{:S(2)}) collective-permute-start(bf16[160,960]{1,0:T(8,128)(2,1)S(1)} %get-tuple-element.88.refs_1_.refs_3_), channel_id=1, source_target_pairs={{1,0},{0,1},{3,2},{2,3},{5,4},{4,5},{7,6},{6,7},{9,8},{8,9},{11,10... | collective-permute-start | bytes 921608 | tf_op jit(solution)/shard_map/ppermute | solution.py:422
  4.8 0.0 collective-permute-start.2
  4.8 1.0 %next_rows.1 = (bf16[128,960]{1,0:T(8,128)(2,1)S(1)}, bf16[128,960]{1,0:T(8,128)(2,1)S(1)}, bf16[128,960]{1,0:T(8,128)(2,1)S(1)}) custom-call(bf16[960,512]{1,0:T(8,128)(2,1)S(1)} %copy-done.2), custom_call_target="tpu_custom_call" | custom-call | flops 1 | bytes 1 | tf_op jit(solution)/shard_map/next_rows/pallas_call | solution.py:313
  5.8 0.1 collective-permute-start.5
  6.0 1.9 %collective-permute-start.4 = (bf16[128,960]{1,0:T(8,128)(2,1)S(1)}, bf16[128,960]{1,0:T(8,128)(2,1)S(1)}, u32[]{:S(2)}, u32[]{:S(2)}) collective-permute-start(bf16[128,960]{1,0:T(8,128)(2,1)S(1)} %get-tuple-element.91.refs_1_), channel_id=1, source_target_pairs={{1,0},{0,1},{3,2},{2,3},{5,4},{4,5},{7,6},{6,7},{9,8},{8,9},{11,10... | collective-permute-start | bytes 737288 | tf_op jit(solution)/shard_map/ppermute | solution.py:422
  7.9 0.1 collective-permute-start
  8.0 0.9 %sqrt_multiply_fusion.refs_6_.refs_7_ = f32[16,960]{1,0:T(8,128)S(1)} fusion(f32[16,960]{1,0:T(8,128)} %param.13, f32[16,960]{1,0:T(8,128)} %refs_6_.9), kind=kLoop, calls=%fused_computation | loop fusion | flops 46080 | bytes 184320 | tf_op jit(solution)/shard_map/mul | solution.py:509
  8.9 0.0 copy-start.1
  8.9 0.0 copy-start.3
  9.0 5.3 %load_weights.1.refs_4_.refs_9_.refs_13_.refs_3_ = bf16[3,1920,960]{2,1,0:T(8,128)(2,1)S(1)} custom-call(bf16[3,960,1920]{2,1,0:T(8,128)(2,1)} %w_hbm), custom_call_target="tpu_custom_call" | custom-call | flops 1 | bytes 1 | tf_op jit(solution)/shard_map/load_weights/pallas_call | solution.py:334
  14.3 2.0 %collective-permute-start.3 = (bf16[16,960]{1,0:T(8,128)(2,1)S(1)}, bf16[16,960]{1,0:T(8,128)(2,1)S(1)}, u32[]{:S(2)}, u32[]{:S(2)}) collective-permute-start(bf16[16,960]{1,0:T(8,128)(2,1)S(1)} %collective-permute-done.2.refs_5_), channel_id=1, source_target_pairs={{1,0},{0,1},{3,2},{2,3},{5,4},{4,5},{7,6},{6,7},{9,8},{8,9},{11,10... | collective-permute-start | bytes 92168 | tf_op jit(solution)/shard_map/ppermute | solution.py:422
  16.3 3.8 %signal_stage.4 = (bf16[528,1920]{1,0:T(8,128)(2,1)S(1)}, f32[512,960]{1,0:T(8,128)S(1)}, f32[4,16,8,960]{3,2,1,0:T(8,128)S(1)}, f32[16,8,960]{2,1,0:T(8,128)S(1)}, f32[2,16,960]{2,1,0:T(8,128)S(1)}) custom-call(s32[2]{0:T(128)S(1)} %pad_add_fusion.refs_0_, bf16[160,960]{1,0:T(8,128)(2,1)S(1)} %get-tuple-element.88.refs_1_.refs_3_, ...), custom_call_target="tpu_custom_call" | custom-call | flops 1 | bytes 1 | tf_op jit(solution)/shard_map/signal_stage/pallas_call | solution.py:313
  20.1 3.5 %signal_stage.5 = (bf16[528,1920]{1,0:T(8,128)(2,1)S(1)}, f32[512,960]{1,0:T(8,128)S(1)}, f32[4,16,8,960]{3,2,1,0:T(8,128)S(1)}, f32[16,8,960]{2,1,0:T(8,128)S(1)}, f32[2,16,960]{2,1,0:T(8,128)S(1)}) custom-call(s32[2]{0:T(128)S(1)} %pad_add_fusion.refs_0_, ...), custom_call_target="tpu_custom_call", output_to_operand_aliasing={{0}: (3, {}), {1}: (4, {}), {2}: (5, {})} | custom-call | flops 1 | bytes 1 | tf_op jit(solution)/shard_map/signal_stage/pallas_call | solution.py:313
  23.6 0.9 %collective-permute-done.4.refs_2_ = bf16[128,960]{1,0:T(8,128)(2,1)S(1)} collective-permute-done((bf16[128,960]{1,0:T(8,128)(2,1)S(1)}, bf16[128,960]{1,0:T(8,128)(2,1)S(1)}, u32[]{:S(2)}, u32[]{:S(2)}) %collective-permute-start.4) | collective-permute-done | bytes 245792 | tf_op jit(solution)/shard_map/ppermute | solution.py:422
  24.6 3.5 %signal_stage.6 = (bf16[528,1920]{1,0:T(8,128)(2,1)S(1)}, f32[512,960]{1,0:T(8,128)S(1)}, f32[4,16,8,960]{3,2,1,0:T(8,128)S(1)}, f32[16,8,960]{2,1,0:T(8,128)S(1)}, f32[2,16,960]{2,1,0:T(8,128)S(1)}) custom-call(s32[2]{0:T(128)S(1)} %pad_add_fusion.refs_0_, ...), custom_call_target="tpu_custom_call", output_to_operand_aliasing={{0}: (3, {}), {1}: (4, {}), {2}: (5, {})} | custom-call | flops 1 | bytes 1 | tf_op jit(solution)/shard_map/signal_stage/pallas_call | solution.py:313
  28.1 2.0 %collective-permute-done.3.refs_6_ = bf16[16,960]{1,0:T(8,128)(2,1)S(1)} collective-permute-done((bf16[16,960]{1,0:T(8,128)(2,1)S(1)}, bf16[16,960]{1,0:T(8,128)(2,1)S(1)}, u32[]{:S(2)}, u32[]{:S(2)}) %collective-permute-start.3) | collective-permute-done | bytes 30752 | tf_op jit(solution)/shard_map/ppermute | solution.py:422
  30.1 4.5 %signal_stage.7 = (bf16[528,1920]{1,0:T(8,128)(2,1)S(1)}, f32[512,960]{1,0:T(8,128)S(1)}, f32[4,16,8,960]{3,2,1,0:T(8,128)S(1)}, f32[16,8,960]{2,1,0:T(8,128)S(1...) custom-call(s32[2]{0:T(128)S(1)} %pad_add_fusion.refs_0_, ...), custom_call_target="tpu_custom_call", output_to_operand_aliasing={{0}: (7, {}), {1}: (8, {}), {2}: (9, {})} | custom-call | flops 1 | bytes 1 | tf_op jit(solution)/shard_map/signal_stage/pallas_call | solution.py:313
  34.6 1.7 %collective-permute-start.7 = (bf16[16,960]{1,0:T(8,128)(2,1)S(1)}, bf16[16,960]{1,0:T(8,128)(2,1)S(1)}, u32[]{:S(2)}, u32[]{:S(2)}) collective-permute-start(bf16[16,960]{1,0:T(8,128)(2,1)S(1)} %get-tuple-element.122), channel_id=1, source_target_pairs={{4,0},{6,2},{0,4},{2,6},{12,8},{14,10},{8,12},{10,14},{20,16},{22,... | collective-permute-start | bytes 92168 | tf_op jit(solution)/shard_map/ppermute | solution.py:468
  36.3 1.4 %collective-permute-start.8 = (bf16[16,960]{1,0:T(8,128)(2,1)S(1)}, bf16[16,960]{1,0:T(8,128)(2,1)S(1)}, u32[]{:S(2)}, u32[]{:S(2)}) collective-permute-start(bf16[16,960]{1,0:T(8,128)(2,1)S(1)} %get-tuple-element.122), channel_id=1, source_target_pairs={{2,0},{4,2},{6,4},{0,6},{10,8},{12,10},{14,12},{8,14},{18,16},{20,... | collective-permute-start | bytes 92168 | tf_op jit(solution)/shard_map/ppermute | solution.py:468
  37.8 0.2 collective-permute-done.6.refs_3_
  37.9 0.6 collective-permute-done.7.refs_4_
  38.5 0.8 %collective-permute-done.8.refs_5_ = bf16[16,960]{1,0:T(8,128)(2,1)S(1)} collective-permute-done((bf16[16,960]{1,0:T(8,128)(2,1)S(1)}, bf16[16,960]{1,0:T(8,128)(2,1)S(1)}, u32[]{:S(2)}, u32[]{:S(2)}) %collective-permute-start.8) | collective-permute-done | bytes 30752 | tf_op jit(solution)/shard_map/ppermute | solution.py:468
  39.4 0.6 combine_states.2
  40.0 2.7 %collective-permute-start.10 = (bf16[16,960]{1,0:T(8,128)(2,1)S(1)}, bf16[16,960]{1,0:T(8,128)(2,1)S(1)}, u32[]{:S(2)}, u32[]{:S(2)}) collective-permute-start(bf16[16,960]{1,0:T(8,128)(2,1)S(1)} %get-tuple-element.124), channel_id=1, source_target_pairs={{16,0},{18,2},{20,4},{22,6},{24,8},{26,10},{28,12},{30,14},{0,16},... | collective-permute-start | bytes 92168 | tf_op jit(solution)/shard_map/ppermute | solution.py:468
  42.7 1.4 %collective-permute-start.11 = (bf16[16,960]{1,0:T(8,128)(2,1)S(1)}, bf16[16,960]{1,0:T(8,128)(2,1)S(1)}, u32[]{:S(2)}, u32[]{:S(2)}) collective-permute-start(bf16[16,960]{1,0:T(8,128)(2,1)S(1)} %get-tuple-element.124), channel_id=1, source_target_pairs={{8,0},{10,2},{12,4},{14,6},{16,8},{18,10},{20,12},{22,14},{24,16},... | collective-permute-start | bytes 92168 | tf_op jit(solution)/shard_map/ppermute | solution.py:468
  44.0 0.7 collective-permute-start.9
  44.7 1.7 %local_stage.4 = (f32[128,960]{1,0:T(8,128)S(1)}, f32[128,960]{1,0:T(8,128)S(1)}, f32[16,8,960]{2,1,0:T(8,128)S(1)}) custom-call(bf16[528,1920]{1,0:T(8,128)(2,1)S(1)} %get-tuple-element.146.refs_0_, f32[512,960]{1,0:T(8,128)S(1)} %get-tuple-element.147.refs_1_, f32[16,8,960]{2,1,0:T(8,128)S(1)} %get-tuple-element.125.refs_2_, ...), custom_call_target="tpu_custom_call" | custom-call | flops 1 | bytes 1 | tf_op jit(solution)/shard_map/local_stage/pallas_call | solution.py:313
  46.4 0.2 collective-permute-done.11.refs_5_
  46.6 3.1 %collective-permute-done.9.refs_3_ = bf16[16,960]{1,0:T(8,128)(2,1)S(1)} collective-permute-done((bf16[16,960]{1,0:T(8,128)(2,1)S(1)}, bf16[16,960]{1,0:T(8,128)(2,1)S(1)}, u32[]{:S(2)}, u32[]{:S(2)}) %collective-permute-start.9) | collective-permute-done | bytes 30752 | tf_op jit(solution)/shard_map/ppermute | solution.py:468
  49.7 0.6 combine_states.3.refs_5_
  50.4 2.5 %second_stage.4 = (bf16[128,960]{1,0:T(8,128)(2,1)S(1)}, f32[128,960]{1,0:T(8,128)S(1)}) custom-call(s32[2]{0:T(128)S(1)} %pad_add_fusion.refs_0_, f32[128,960]{1,0:T(8,128)S(1)} %get-tuple-element.135.refs_1_, f32[128,960]{1,0:T(8,128)S(1)} %get-tuple-element.136.refs_2_, f32[16,8,960]{2,1,0:T(8,128)S(1)} %get-tuple-element.137.refs_3_, ...), custom_call_target="tpu_custom_call" | custom-call | flops 1 | bytes 1 | tf_op jit(solution)/shard_map/second_stage/pallas_call | solution.py:313
  52.9 1.6 %collective-permute-start.12 = (bf16[128,960]{1,0:T(8,128)(2,1)S(1)}, bf16[128,960]{1,0:T(8,128)(2,1)S(1)}, u32[]{:S(2)}, u32[]{:S(2)}) collective-permute-start(bf16[128,960]{1,0:T(8,128)(2,1)S(1)} %get-tuple-element.139), channel_id=1, source_target_pairs={{1,0},{0,1},{3,2},{2,3},{5,4},{4,5},{7,6},{6,7},{9,8},{8,9},{11,10... | collective-permute-start | bytes 737288 | tf_op jit(solution)/shard_map/ppermute | solution.py:422
  54.5 1.3 %local_stage.5 = (f32[128,960]{1,0:T(8,128)S(1)}, f32[128,960]{1,0:T(8,128)S(1)}) custom-call(bf16[528,1920]{1,0:T(8,128)(2,1)S(1)} %get-tuple-element.146.refs_0_, f32[512,960]{1,0:T(8,128)S(1)} %get-tuple-element.147.refs_1_, f32[16,8,960]{2,1,0:T(8,128)S(1)} %get-tuple-element.125.refs_2_, ...), custom_call_target="tpu_custom_call" | custom-call | flops 1 | bytes 1 | tf_op jit(solution)/shard_map/local_stage/pallas_call | solution.py:313
  55.8 2.4 %second_stage.5 = (bf16[128,960]{1,0:T(8,128)(2,1)S(1)}, f32[128,960]{1,0:T(8,128)S(1)}) custom-call(s32[2]{0:T(128)S(1)} %pad_add_fusion.refs_0_, f32[128,960]{1,0:T(8,128)S(1)} %get-tuple-element.143.refs_1_, f32[128,960]{1,0:T(8,128)S(1)} %get-tuple-element.144.refs_2_, f32[16,8,960]{2,1,0:T(8,128)S(1)} %get-tuple-element.137.refs_3_, ...), custom_call_target="tpu_custom_call" | custom-call | flops 1 | bytes 1 | tf_op jit(solution)/shard_map/second_stage/pallas_call | solution.py:313
  58.2 0.6 collective-permute-start.13
  58.8 1.9 %collective-permute-done.12.refs_3_ = bf16[128,960]{1,0:T(8,128)(2,1)S(1)} collective-permute-done((bf16[128,960]{1,0:T(8,128)(2,1)S(1)}, bf16[128,960]{1,0:T(8,128)(2,1)S(1)}, u32[]{:S(2)}, u32[]{:S(2)}) %collective-permute-start.12) | collective-permute-done | bytes 245792 | tf_op jit(solution)/shard_map/ppermute | solution.py:422
  60.7 1.3 %local_stage.7 = (f32[128,960]{1,0:T(8,128)S(1)}, f32[128,960]{1,0:T(8,128)S(1)}) custom-call(bf16[528,1920]{1,0:T(8,128)(2,1)S(1)} %get-tuple-element.146.refs_0_, f32[512,960]{1,0:T(8,128)S(1)} %get-tuple-element.147.refs_1_, f32[16,8,960]{2,1,0:T(8,128)S(1)} %get-tuple-element.125.refs_2_, ...), custom_call_target="tpu_custom_call" | custom-call | flops 1 | bytes 1 | tf_op jit(solution)/shard_map/local_stage/pallas_call | solution.py:313
  62.0 2.5 %second_stage.7 = (bf16[128,960]{1,0:T(8,128)(2,1)S(1)}, f32[128,960]{1,0:T(8,128)S(1)}) custom-call(s32[2]{0:T(128)S(1)} %pad_add_fusion.refs_0_, f32[128,960]{1,0:T(8,128)S(1)} %get-tuple-element.155.refs_1_, f32[128,960]{1,0:T(8,128)S(1)} %get-tuple-element.156.refs_2_, f32[16,8,960]{2,1,0:T(8,128)S(1)} %get-tuple-element.137.refs_3_, ...), custom_call_target="tpu_custom_call" | custom-call | flops 1 | bytes 1 | tf_op jit(solution)/shard_map/second_stage/pallas_call | solution.py:313
  64.5 2.5 %collective-permute-start.15 = (bf16[128,960]{1,0:T(8,128)(2,1)S(1)}, bf16[128,960]{1,0:T(8,128)(2,1)S(1)}, u32[]{:S(2)}, u32[]{:S(2)}) collective-permute-start(bf16[128,960]{1,0:T(8,128)(2,1)S(1)} %get-tuple-element.160), channel_id=1, source_target_pairs={{1,0},{0,1},{3,2},{2,3},{5,4},{4,5},{7,6},{6,7},{9,8},{8,9},{11,10... | collective-permute-start | bytes 737288 | tf_op jit(solution)/shard_map/ppermute | solution.py:422
  67.0 1.3 %local_stage.6 = (f32[128,960]{1,0:T(8,128)S(1)}, f32[128,960]{1,0:T(8,128)S(1)}) custom-call(bf16[528,1920]{1,0:T(8,128)(2,1)S(1)} %get-tuple-element.146.refs_0_, f32[512,960]{1,0:T(8,128)S(1)} %get-tuple-element.147.refs_1_, f32[16,8,960]{2,1,0:T(8,128)S(1)} %get-tuple-element.125.refs_2_, ...), custom_call_target="tpu_custom_call" | custom-call | flops 1 | bytes 1 | tf_op jit(solution)/shard_map/local_stage/pallas_call | solution.py:313
  68.3 2.5 %second_stage.6 = (bf16[128,960]{1,0:T(8,128)(2,1)S(1)}, f32[128,960]{1,0:T(8,128)S(1)}) custom-call(s32[2]{0:T(128)S(1)} %pad_add_fusion.refs_0_, f32[128,960]{1,0:T(8,128)S(1)} %get-tuple-element.148.refs_1_, f32[128,960]{1,0:T(8,128)S(1)} %get-tuple-element.149.refs_2_, f32[16,8,960]{2,1,0:T(8,128)S(1)} %get-tuple-element.137.refs_3_, ...), custom_call_target="tpu_custom_call" | custom-call | flops 1 | bytes 1 | tf_op jit(solution)/shard_map/second_stage/pallas_call | solution.py:313
  70.8 1.4 %collective-permute-start.14 = (bf16[128,960]{1,0:T(8,128)(2,1)S(1)}, bf16[128,960]{1,0:T(8,128)(2,1)S(1)}, u32[]{:S(2)}, u32[]{:S(2)}) collective-permute-start(bf16[128,960]{1,0:T(8,128)(2,1)S(1)} %get-tuple-element.152), channel_id=1, source_target_pairs={{1,0},{0,1},{3,2},{2,3},{5,4},{4,5},{7,6},{6,7},{9,8},{8,9},{11,10... | collective-permute-start | bytes 737288 | tf_op jit(solution)/shard_map/ppermute | solution.py:422
  72.2 0.7 last_stage.2.refs_2_
  73.0 4.3 %collective-permute-done.14.refs_1_ = bf16[128,960]{1,0:T(8,128)(2,1)S(1)} collective-permute-done((bf16[128,960]{1,0:T(8,128)(2,1)S(1)}, bf16[128,960]{1,0:T(8,128)(2,1)S(1)}, u32[]{:S(2)}, u32[]{:S(2)}) %collective-permute-start.14) | collective-permute-done | bytes 245792 | tf_op jit(solution)/shard_map/ppermute | solution.py:422
  77.3 1.4 %last_stage.3 = bf16[960,512]{1,0:T(8,128)(2,1)} custom-call(f32[128,960]{1,0:T(8,128)S(1)} %get-tuple-element.151.refs_0_, bf16[128,960]{1,0:T(8,128)(2,1)S(1)} %collective-permute-done.14.refs_1_, f32[960,512]{1,0:T(8,128)S(1)} %last_stage.2.refs_2_), custom_call_target="tpu_custom_call" | custom-call | flops 1 | bytes 1 | tf_op jit(solution)/shard_map/last_stage/pallas_call | solution.py:313
  (18 shorter events, 0.0 us)
Async XLA Ops:
  0.0 8.9 %copy-start.5 = (f32[1920]{0:T(1024)S(1)}, f32[1920]{0:T(1024)}, u32[]{:S(2)}) copy-start(f32[1920]{0:T(1024)} %param.9) | copy-start | bytes 23044
  0.1 1.2 %copy-start.2 = (bf16[960,512]{1,0:T(8,128)(2,1)S(1)}, bf16[960,512]{1,0:T(8,128)(2,1)}, u32[]{:S(2)}) copy-start(bf16[960,512]{1,0:T(8,128)(2,1)} %tokens_ref.1) | copy-start | bytes 2949124
  1.8 14.6 %collective-permute-start.1 = (bf16[160,960]{1,0:T(8,128)(2,1)S(1)}, bf16[160,960]{1,0:T(8,128)(2,1)S(1)}, u32[]{:S(2)}, u32[]{:S(2)}) collective-permute-start(bf16[160,960]{1,0:T(8,128)(2,1)S(1)} %get-tuple-element.88.refs_1_.refs_3_), channel_id=1, source_target_pairs={{1,0},{0,1},{3,2},{2,3},{5,4},{4,5},{7,6},{6,7},{9,8},{8,9},{11,10... | collective-permute-start | bytes 921608 | tf_op jit(solution)/shard_map/ppermute | solution.py:422
  4.8 9.5 %collective-permute-start.2 = (bf16[16,960]{1,0:T(8,128)(2,1)S(1)}, bf16[16,960]{1,0:T(8,128)(2,1)S(1)}, u32[]{:S(2)}, u32[]{:S(2)}) collective-permute-start(bf16[16,960]{1,0:T(8,128)(2,1)S(1)} %get-tuple-element.89), channel_id=1, source_target_pairs={{30,0},{0,2},{2,4},{4,6},{6,8},{8,10},{10,12},{12,14},{14,16},{16,... | collective-permute-start | bytes 92168 | tf_op jit(solution)/shard_map/ppermute | solution.py:422
  5.8 14.3 %collective-permute-start.5 = (bf16[128,960]{1,0:T(8,128)(2,1)S(1)}, bf16[128,960]{1,0:T(8,128)(2,1)S(1)}, u32[]{:S(2)}, u32[]{:S(2)}) collective-permute-start(bf16[128,960]{1,0:T(8,128)(2,1)S(1)} %get-tuple-element.90.refs_1_), channel_id=1, source_target_pairs={{1,0},{0,1},{3,2},{2,3},{5,4},{4,5},{7,6},{6,7},{9,8},{8,9},{11,10... | collective-permute-start | bytes 737288 | tf_op jit(solution)/shard_map/ppermute | solution.py:422
  6.0 18.6 %collective-permute-start.4 = (bf16[128,960]{1,0:T(8,128)(2,1)S(1)}, bf16[128,960]{1,0:T(8,128)(2,1)S(1)}, u32[]{:S(2)}, u32[]{:S(2)}) collective-permute-start(bf16[128,960]{1,0:T(8,128)(2,1)S(1)} %get-tuple-element.91.refs_1_), channel_id=1, source_target_pairs={{1,0},{0,1},{3,2},{2,3},{5,4},{4,5},{7,6},{6,7},{9,8},{8,9},{11,10... | collective-permute-start | bytes 737288 | tf_op jit(solution)/shard_map/ppermute | solution.py:422
  7.9 22.1 %collective-permute-start = (bf16[128,960]{1,0:T(8,128)(2,1)S(1)}, bf16[128,960]{1,0:T(8,128)(2,1)S(1)}, u32[]{:S(2)}, u32[]{:S(2)}) collective-permute-start(bf16[128,960]{1,0:T(8,128)(2,1)S(1)} %get-tuple-element.87.refs_1_), channel_id=1, source_target_pairs={{1,0},{0,1},{3,2},{2,3},{5,4},{4,5},{7,6},{6,7},{9,8},{8,9},{11,10... | collective-permute-start | bytes 737288 | tf_op jit(solution)/shard_map/ppermute | solution.py:422
  8.9 7.4 %copy-start.1 = (f32[16,960]{1,0:T(8,128)S(1)}, f32[16,960]{1,0:T(8,128)}, u32[]{:S(2)}) copy-start(f32[16,960]{1,0:T(8,128)} %refs_6_.9) | copy-start | bytes 184324
  8.9 7.4 %copy-start.3 = (f32[3,3,960]{2,1,0:T(4,128)S(1)}, f32[3,3,960]{2,1,0:T(4,128)}, u32[]{:S(2)}) copy-start(f32[3,3,960]{2,1,0:T(4,128)} %refs_4_.7) | copy-start | bytes 103684
  14.3 15.8 %collective-permute-start.3 = (bf16[16,960]{1,0:T(8,128)(2,1)S(1)}, bf16[16,960]{1,0:T(8,128)(2,1)S(1)}, u32[]{:S(2)}, u32[]{:S(2)}) collective-permute-start(bf16[16,960]{1,0:T(8,128)(2,1)S(1)} %collective-permute-done.2.refs_5_), channel_id=1, source_target_pairs={{1,0},{0,1},{3,2},{2,3},{5,4},{4,5},{7,6},{6,7},{9,8},{8,9},{11,10... | collective-permute-start | bytes 92168 | tf_op jit(solution)/shard_map/ppermute | solution.py:422
  30.1 14.7 %copy-start.4 = (f32[960]{0:T(1024)S(1)}, f32[960]{0:T(1024)}, u32[]{:S(2)}) copy-start(f32[960]{0:T(1024)} %param.14) | copy-start | bytes 11524
  34.6 3.3 %collective-permute-start.6 = (bf16[16,960]{1,0:T(8,128)(2,1)S(1)}, bf16[16,960]{1,0:T(8,128)(2,1)S(1)}, u32[]{:S(2)}, u32[]{:S(2)}) collective-permute-start(bf16[16,960]{1,0:T(8,128)(2,1)S(1)} %get-tuple-element.122), channel_id=1, source_target_pairs={{6,0},{0,2},{2,4},{4,6},{14,8},{8,10},{10,12},{12,14},{22,16},{16,... | collective-permute-start | bytes 92168 | tf_op jit(solution)/shard_map/ppermute | solution.py:468
  34.6 3.9 %collective-permute-start.7 = (bf16[16,960]{1,0:T(8,128)(2,1)S(1)}, bf16[16,960]{1,0:T(8,128)(2,1)S(1)}, u32[]{:S(2)}, u32[]{:S(2)}) collective-permute-start(bf16[16,960]{1,0:T(8,128)(2,1)S(1)} %get-tuple-element.122), channel_id=1, source_target_pairs={{4,0},{6,2},{0,4},{2,6},{12,8},{14,10},{8,12},{10,14},{20,16},{22,... | collective-permute-start | bytes 92168 | tf_op jit(solution)/shard_map/ppermute | solution.py:468
  36.3 3.0 %collective-permute-start.8 = (bf16[16,960]{1,0:T(8,128)(2,1)S(1)}, bf16[16,960]{1,0:T(8,128)(2,1)S(1)}, u32[]{:S(2)}, u32[]{:S(2)}) collective-permute-start(bf16[16,960]{1,0:T(8,128)(2,1)S(1)} %get-tuple-element.122), channel_id=1, source_target_pairs={{2,0},{4,2},{6,4},{0,6},{10,8},{12,10},{14,12},{8,14},{18,16},{20,... | collective-permute-start | bytes 92168 | tf_op jit(solution)/shard_map/ppermute | solution.py:468
  40.0 6.4 %collective-permute-start.10 = (bf16[16,960]{1,0:T(8,128)(2,1)S(1)}, bf16[16,960]{1,0:T(8,128)(2,1)S(1)}, u32[]{:S(2)}, u32[]{:S(2)}) collective-permute-start(bf16[16,960]{1,0:T(8,128)(2,1)S(1)} %get-tuple-element.124), channel_id=1, source_target_pairs={{16,0},{18,2},{20,4},{22,6},{24,8},{26,10},{28,12},{30,14},{0,16},... | collective-permute-start | bytes 92168 | tf_op jit(solution)/shard_map/ppermute | solution.py:468
  42.7 3.9 %collective-permute-start.11 = (bf16[16,960]{1,0:T(8,128)(2,1)S(1)}, bf16[16,960]{1,0:T(8,128)(2,1)S(1)}, u32[]{:S(2)}, u32[]{:S(2)}) collective-permute-start(bf16[16,960]{1,0:T(8,128)(2,1)S(1)} %get-tuple-element.124), channel_id=1, source_target_pairs={{8,0},{10,2},{12,4},{14,6},{16,8},{18,10},{20,12},{22,14},{24,16},... | collective-permute-start | bytes 92168 | tf_op jit(solution)/shard_map/ppermute | solution.py:468
  44.0 5.7 %collective-permute-start.9 = (bf16[16,960]{1,0:T(8,128)(2,1)S(1)}, bf16[16,960]{1,0:T(8,128)(2,1)S(1)}, u32[]{:S(2)}, u32[]{:S(2)}) collective-permute-start(bf16[16,960]{1,0:T(8,128)(2,1)S(1)} %get-tuple-element.124), channel_id=1, source_target_pairs={{24,0},{26,2},{28,4},{30,6},{0,8},{2,10},{4,12},{6,14},{8,16},{10,... | collective-permute-start | bytes 92168 | tf_op jit(solution)/shard_map/ppermute | solution.py:468
  44.7 5.6 %copy-start = (bf16[960,1920]{1,0:T(8,128)(2,1)S(1)}, bf16[960,1920]{1,0:T(8,128)(2,1)}, u32[]{:S(2)}) copy-start(bf16[960,1920]{1,0:T(8,128)(2,1)} %refs_8_.7) | copy-start | bytes 11059204
  52.9 7.8 %collective-permute-start.12 = (bf16[128,960]{1,0:T(8,128)(2,1)S(1)}, bf16[128,960]{1,0:T(8,128)(2,1)S(1)}, u32[]{:S(2)}, u32[]{:S(2)}) collective-permute-start(bf16[128,960]{1,0:T(8,128)(2,1)S(1)} %get-tuple-element.139), channel_id=1, source_target_pairs={{1,0},{0,1},{3,2},{2,3},{5,4},{4,5},{7,6},{6,7},{9,8},{8,9},{11,10... | collective-permute-start | bytes 737288 | tf_op jit(solution)/shard_map/ppermute | solution.py:422
  58.2 8.8 %collective-permute-start.13 = (bf16[128,960]{1,0:T(8,128)(2,1)S(1)}, bf16[128,960]{1,0:T(8,128)(2,1)S(1)}, u32[]{:S(2)}, u32[]{:S(2)}) collective-permute-start(bf16[128,960]{1,0:T(8,128)(2,1)S(1)} %get-tuple-element.145), channel_id=1, source_target_pairs={{1,0},{0,1},{3,2},{2,3},{5,4},{4,5},{7,6},{6,7},{9,8},{8,9},{11,10... | collective-permute-start | bytes 737288 | tf_op jit(solution)/shard_map/ppermute | solution.py:422
  64.5 7.8 %collective-permute-start.15 = (bf16[128,960]{1,0:T(8,128)(2,1)S(1)}, bf16[128,960]{1,0:T(8,128)(2,1)S(1)}, u32[]{:S(2)}, u32[]{:S(2)}) collective-permute-start(bf16[128,960]{1,0:T(8,128)(2,1)S(1)} %get-tuple-element.160), channel_id=1, source_target_pairs={{1,0},{0,1},{3,2},{2,3},{5,4},{4,5},{7,6},{6,7},{9,8},{8,9},{11,10... | collective-permute-start | bytes 737288 | tf_op jit(solution)/shard_map/ppermute | solution.py:422
  70.8 6.4 %collective-permute-start.14 = (bf16[128,960]{1,0:T(8,128)(2,1)S(1)}, bf16[128,960]{1,0:T(8,128)(2,1)S(1)}, u32[]{:S(2)}, u32[]{:S(2)}) collective-permute-start(bf16[128,960]{1,0:T(8,128)(2,1)S(1)} %get-tuple-element.152), channel_id=1, source_target_pairs={{1,0},{0,1},{3,2},{2,3},{5,4},{4,5},{7,6},{6,7},{9,8},{8,9},{11,10... | collective-permute-start | bytes 737288 | tf_op jit(solution)/shard_map/ppermute | solution.py:422
